TPU v7x, 128 devices: a whole 4x4x4 slice. The times are simulated.
128 devices in a mesh: wide: 16 (over z, x_lo, core), narrow: 8 (over y, x_hi).
Axes of the slice: x: 4 (x_hi: 2, x_lo: 2; x = x_hi * 2 + x_lo), y: 4, z: 4, core: 2. Of those that a mesh axis runs over, the one named last changes fastest.
Arguments:
- tokens: bfloat16 [16384, 7168], P(('wide', 'narrow')), may hold values from -6 to 6
- grad_out: bfloat16 [16384, 7168], P(('wide', 'narrow')), may hold values from -2.5 to 2.5
- gates: bfloat16 [16384, 8], P(('wide', 'narrow')), may hold values from 0.099609375 to 1
- expert_ids: int32 [16384, 8], P(('wide', 'narrow')), may hold values from 0 to 255, as said below
- slots: int32 [16384, 8], P(('wide', 'narrow')), may hold values from 0 to 4, as said below
- w_gate: bfloat16 [16, 1792, 7168], P('wide', 'narrow'), may hold values from -0.0625 to 0.0625
- w_up: bfloat16 [16, 1792, 7168], P('wide', 'narrow'), may hold values from -0.0625 to 0.0625
- w_down: bfloat16 [16, 1792, 7168], P('wide', 'narrow'), may hold values from -0.125 to 0.125
Outputs:
- grad_tokens: bfloat16 [16384, 7168], P(('wide', 'narrow'))
- grad_gates: float32 [16384, 8], P(('wide', 'narrow'))
- grad_w_gate: bfloat16 [16, 1792, 7168], P('wide', 'narrow')
- grad_w_up: bfloat16 [16, 1792, 7168], P('wide', 'narrow')
- grad_w_down: bfloat16 [16, 1792, 7168], P('wide', 'narrow')
Inputs may be any that keep to these rules, and one draw needn't show every extreme that they name: `expert_ids`: each row names 8 different experts. `slots`: for a pair whose expert is below 16, the slot is the smaller of 4 and the number of earlier pairs (row-major over token and k) of the same device's tokens with the same expert; every other pair has slot 4; slot 4 marks a pair that is not kept, so no two kept pairs of one device share an expert and a slot.
All inputs are finite; a program needn't handle non-finite values.
Results may differ from a plain program's by a relative error of at most 0.0057.
Values may be sent and summed in bfloat16 or wider, within the bound.
A program may use at most 576 MiB of HBM per device.

v0:
```python
import jax
import jax.numpy as jnp
from jax import lax
from jax.sharding import PartitionSpec as P

CAP = 4


def project(rows, weight):
    return lax.dot_general(
        rows, weight, (((1,), (1,)), ((), ())), preferred_element_type=jnp.float32
    )


def outer_sum(left, right):
    return lax.dot_general(
        left, right, (((0,), (0,)), ((), ())), preferred_element_type=jnp.float32
    )


def hidden_grads(rows_input, rows_grad, rows_weight, weight_gate, weight_up, weight_down):
    pre_gate = project(rows_input, weight_gate)
    pre_up = project(rows_input, weight_up)
    back_down = project(rows_grad, weight_down)
    sigmoid_gate = jax.nn.sigmoid(pre_gate)
    active = pre_gate * sigmoid_gate
    scaled = rows_weight[:, None] * back_down
    grad_gate = (scaled * pre_up * sigmoid_gate * (1.0 + pre_gate * (1.0 - sigmoid_gate))).astype(
        jnp.bfloat16
    )
    grad_up = (scaled * active).astype(jnp.bfloat16)
    hidden = (active * pre_up).astype(jnp.bfloat16)
    gate_part = jnp.sum(back_down * active * pre_up, axis=1)
    input_part = jnp.dot(grad_gate, weight_gate, preferred_element_type=jnp.float32) + jnp.dot(
        grad_up, weight_up, preferred_element_type=jnp.float32
    )
    scaled_grad = (rows_weight[:, None] * rows_grad.astype(jnp.float32)).astype(jnp.bfloat16)
    return (grad_gate, grad_up, hidden, scaled_grad, input_part, gate_part)


def per_device(tokens, grad_out, gates, expert_ids, slots, w_gate, w_up, w_down):
    n_wide = lax.axis_size("wide")
    n_narrow = lax.axis_size("narrow")
    model_width = tokens.shape[1]
    slot_count = n_wide * CAP
    kept_pair = (expert_ids < n_wide) & (slots < CAP)
    target = jnp.where(kept_pair, expert_ids * CAP + slots, slot_count)
    picked = (target[:, :, None] == jnp.arange(slot_count, dtype=jnp.int32)[None, None, :]).astype(
        jnp.float32
    )
    placing = jnp.sum(picked, axis=1)
    placing_b = placing.astype(jnp.bfloat16)
    send_input = outer_sum(placing_b, tokens).astype(jnp.bfloat16).reshape(n_wide, CAP, model_width)
    send_grad = (
        outer_sum(placing_b, grad_out).astype(jnp.bfloat16).reshape(n_wide, CAP, model_width)
    )
    send_weight = (
        jnp.einsum("tkl,tk->l", picked, gates.astype(jnp.float32), precision=lax.Precision.HIGHEST)
        .astype(jnp.bfloat16)
        .reshape(n_wide, CAP)
    )
    copy_shape = (n_wide * n_narrow, CAP, model_width)
    fanned_input = jnp.broadcast_to(
        send_input[:, None], (n_wide, n_narrow, CAP, model_width)
    ).reshape(copy_shape)
    fanned_grad = jnp.broadcast_to(
        send_grad[:, None], (n_wide, n_narrow, CAP, model_width)
    ).reshape(copy_shape)
    fanned_weight = jnp.broadcast_to(send_weight[:, None], (n_wide, n_narrow, CAP)).reshape(
        n_wide * n_narrow, CAP
    )
    recv_input, recv_grad, recv_weight = (
        lax.all_to_all(fanned_input, ("wide", "narrow"), split_axis=0, concat_axis=0, tiled=True),
        lax.all_to_all(fanned_grad, ("wide", "narrow"), split_axis=0, concat_axis=0, tiled=True),
        lax.all_to_all(fanned_weight, ("wide", "narrow"), split_axis=0, concat_axis=0, tiled=True),
    )
    rows_input = recv_input.reshape(-1, model_width)
    grad_gate, grad_up, hidden, scaled_grad, input_part, gate_part = hidden_grads(
        rows_input,
        recv_grad.reshape(-1, model_width),
        recv_weight.reshape(-1).astype(jnp.float32),
        w_gate[0],
        w_up[0],
        w_down[0],
    )
    sum_gate = outer_sum(grad_gate, rows_input)
    sum_up = outer_sum(grad_up, rows_input)
    sum_down = outer_sum(hidden, scaled_grad)
    back_input, back_gate = (
        lax.all_to_all(
            input_part.reshape(copy_shape),
            ("wide", "narrow"),
            split_axis=0,
            concat_axis=0,
            tiled=True,
        ),
        lax.all_to_all(
            gate_part.reshape(n_wide * n_narrow, CAP),
            ("wide", "narrow"),
            split_axis=0,
            concat_axis=0,
            tiled=True,
        ),
    )
    pair_input = jnp.sum(back_input.reshape(n_wide, n_narrow, CAP, model_width), axis=1)
    pair_gate = jnp.sum(back_gate.reshape(n_wide, n_narrow, CAP), axis=1)
    grad_tokens = jnp.dot(
        placing,
        pair_input.reshape(slot_count, model_width),
        precision=lax.Precision.HIGHEST,
        preferred_element_type=jnp.float32,
    ).astype(jnp.bfloat16)
    grad_gates = jnp.einsum(
        "tkl,l->tk", picked, pair_gate.reshape(slot_count), precision=lax.Precision.HIGHEST
    )
    grad_w_gate = sum_gate[None].astype(jnp.bfloat16)
    grad_w_up = sum_up[None].astype(jnp.bfloat16)
    grad_w_down = sum_down[None].astype(jnp.bfloat16)
    return (grad_tokens, grad_gates, grad_w_gate, grad_w_up, grad_w_down)


def solution(mesh):
    placed = (
        P(("wide", "narrow"), None),
        P(("wide", "narrow"), None),
        P(("wide", "narrow"), None),
        P(("wide", "narrow"), None),
        P(("wide", "narrow"), None),
        P("wide", "narrow", None),
        P("wide", "narrow", None),
        P("wide", "narrow", None),
    )
    return jax.shard_map(
        per_device,
        mesh=mesh,
        in_specs=placed,
        out_specs=(
            P(("wide", "narrow"), None),
            P(("wide", "narrow"), None),
            P("wide", "narrow", None),
            P("wide", "narrow", None),
            P("wide", "narrow", None),
        ),
        check_vma=False,
    )
```

profile of v0, /device:TPU:1, one launch (start us, length us, event | category | flops | bytes accessed | tf_op | source)
XLA Modules:
  0.0 502.9 jit_solution(6334536585140873159)
XLA Ops:
  0.6 0.0 copy-start
  0.6 0.9 add_select_fusion
  1.5 1.0 fusion.13
  2.5 0.1 broadcast_in_dim.17
  2.6 0.1 copy.21
  2.7 0.1 broadcast_in_dim.34
  2.7 0.1 all_to_all.21
  2.9 0.8 copy.22
  3.6 11.5 %all-to-all-start = ((bf16[128,1,4]{2,1,0:T(2,128)(2,1)}), bf16[128,1,4]{2,1,0:T(2,128)(2,1)S(1)}, u32[]{:S(2)}, u32[]{:S(2)}) async-start(bf16[128,1,4]{2,1,0:T(2,128)(2,1)} %copy.22), calls=%async_computation | async-start | bytes 131072 | tf_op jit(solution)/shard_map/all_to_all | solution.py:75
  15.2 2.8 convolution_convert_fusion.5
  18.0 2.5 broadcast_in_dim.35
  20.5 4.4 all-to-all-done
  25.0 6.4 %broadcast_in_dim.36 = bf16[16,8,4,7168]{3,2,1,0:T(4,128)(2,1)} broadcast(bf16[16,4,7168]{2,1,0:T(4,128)(2,1)} %broadcast_in_dim.35), dimensions={0,2,3} | broadcast | bytes 8257536 | tf_op jit(solution)/shard_map/broadcast_in_dim | solution.py:66
  31.3 5.7 %all-to-all-start.1 = ((bf16[128,4,7168]{2,1,0:T(4,128)(2,1)}), bf16[128,4,7168]{2,1,0:T(4,128)(2,1)}, u32[]{:S(2)}, u32[]{:S(2)}) async-start(bf16[128,4,7168]{2,1,0:T(4,128)(2,1)} %bitcast.54), calls=%async_computation.1 | async-start | bytes 14680064 | tf_op jit(solution)/shard_map/all_to_all | solution.py:74
  37.1 2.8 convolution_convert_fusion.4
  39.9 2.5 broadcast_in_dim.37
  42.4 82.6 %all-to-all-done.1 = bf16[128,4,7168]{2,1,0:T(4,128)(2,1)} async-done(((bf16[128,4,7168]{2,1,0:T(4,128)(2,1)}), bf16[128,4,7168]{2,1,0:T(4,128)(2,1)}, u32[]{:S(2)}, u32[]{:S(2)}) %all-to-all-start.1) | async-done | bytes 7340064 | tf_op jit(solution)/shard_map/all_to_all | solution.py:74
  125.0 6.3 %broadcast_in_dim.38 = bf16[16,8,4,7168]{3,2,1,0:T(4,128)(2,1)} broadcast(bf16[16,4,7168]{2,1,0:T(4,128)(2,1)} %broadcast_in_dim.37), dimensions={0,2,3} | broadcast | bytes 8257536 | tf_op jit(solution)/shard_map/broadcast_in_dim | solution.py:63
  131.3 7.8 %all-to-all-start.2 = ((bf16[128,4,7168]{2,1,0:T(4,128)(2,1)}), bf16[128,4,7168]{2,1,0:T(4,128)(2,1)}, u32[]{:S(2)}, u32[]{:S(2)}) async-start(bf16[128,4,7168]{2,1,0:T(4,128)(2,1)} %bitcast.53), calls=%async_computation.2 | async-start | bytes 14680064 | tf_op jit(solution)/shard_map/all_to_all | solution.py:73
  139.1 0.2 convert_reduce_fusion.1
  139.3 0.1 reshape.71
  139.4 12.1 %reshape.63 = bf16[512,7168]{1,0:T(8,128)(2,1)} reshape(bf16[128,4,7168]{2,1,0:T(4,128)(2,1)} %all-to-all-done.1) | data formatting | bytes 14680064 | tf_op jit(solution)/shard_map/reshape | solution.py:80
  151.5 7.1 %fusion.11 = f32[512,224]{0,1:T(8,128)} fusion(bf16[512,7168]{1,0:T(8,128)(2,1)} %reshape.63, bf16[1,224,7168]{2,1,0:T(8,128)(2,1)} %param.15), kind=kOutput, calls=%fused_computation.20 | convolution fusion | flops 1644167168 | bytes 11010048 | tf_op jit(solution)/shard_map/dot_general | solution.py:10
  158.6 68.5 %all-to-all-done.2 = bf16[128,4,7168]{2,1,0:T(4,128)(2,1)} async-done(((bf16[128,4,7168]{2,1,0:T(4,128)(2,1)}), bf16[128,4,7168]{2,1,0:T(4,128)(2,1)}, u32[]{:S(2)}, u32[]{:S(2)}) %all-to-all-start.2) | async-done | bytes 7340064 | tf_op jit(solution)/shard_map/all_to_all | solution.py:73
  227.1 12.1 %reshape.65 = bf16[512,7168]{1,0:T(8,128)(2,1)} reshape(bf16[128,4,7168]{2,1,0:T(4,128)(2,1)} %all-to-all-done.2) | data formatting | bytes 14680064 | tf_op jit(solution)/shard_map/reshape | solution.py:77
  239.2 0.0 copy-start.2
  239.2 0.0 copy-start.6
  239.2 6.5 %fusion.6 = f32[512,224]{0,1:T(8,128)S(1)} fusion(bf16[512,7168]{1,0:T(8,128)(2,1)} %reshape.65, bf16[1,224,7168]{2,1,0:T(8,128)(2,1)} %param.13), kind=kOutput, calls=%fused_computation.15 | convolution fusion | flops 1644167168 | bytes 11010048 | tf_op jit(solution)/shard_map/dot_general | solution.py:10
  245.7 0.0 copy-done
  245.8 0.0 copy-done.2
  245.8 0.0 copy-done.6
  245.8 0.0 copy-start.4
  245.8 3.3 multiply_reduce_fusion
  249.1 0.0 copy-done.4
  249.1 0.7 all_to_all.26
  249.8 7.0 %all-to-all-start.4 = ((f32[128,1,4]{2,1,0:T(1,128)}), f32[128,1,4]{2,1,0:T(1,128)S(1)}, u32[]{:S(2)}, u32[]{:S(2)}) async-start(f32[128,1,4]{2,1,0:T(1,128)} %bitcast.58), calls=%async_computation.4 | async-start | bytes 131072 | tf_op jit(solution)/shard_map/all_to_all | solution.py:97
  256.8 4.2 fusion.4
  261.0 7.4 %convolution_add_fusion = f32[512,7168]{1,0:T(8,128)} fusion(f32[512,7168]{1,0:T(8,128)S(1)} %fusion.4, bf16[512,224]{0,1:T(8,128)(2,1)S(1)} %get-tuple-element.7, bf16[1,224,7168]{2,1,0:T(8,128)(2,1)S(1)} %copy-done), kind=kOutput, calls=%fused_computation.2 | convolution fusion | flops 1647837184 | bytes 32800768 | tf_op jit(solution)/shard_map/dot_general | solution.py:34
  268.4 17.0 %reshape.66 = f32[128,4,7168]{2,1,0:T(4,128)} reshape(f32[512,7168]{1,0:T(8,128)} %convolution_add_fusion) | data formatting | bytes 29360128 | tf_op jit(solution)/shard_map/reshape | solution.py:91
  285.4 0.0 copy-start.3
  285.4 0.0 all-to-all-done.4
  285.4 10.2 %all-to-all-start.3 = ((f32[128,4,7168]{2,1,0:T(4,128)}), f32[128,4,7168]{2,1,0:T(4,128)}, u32[]{:S(2)}, u32[]{:S(2)}) async-start(f32[128,4,7168]{2,1,0:T(4,128)} %reshape.66), calls=%async_computation.3 | async-start | bytes 29360128 | tf_op jit(solution)/shard_map/all_to_all | solution.py:90
  295.6 0.0 copy-done.3
  295.6 0.0 slice-start
  295.6 6.8 %fusion = bf16[1,224,7168]{2,1,0:T(8,128)(2,1)} fusion(bf16[512,224]{0,1:T(8,128)(2,1)S(1)} %copy-done.3, bf16[512,7168]{1,0:T(8,128)(2,1)} %reshape.65), kind=kOutput, calls=%fused_computation.6 | convolution fusion | flops 1645772800 | bytes 10780672 | tf_op jit(solution)/shard_map/dot_general | solution.py:16
  302.3 0.0 slice-start.1
  302.3 0.0 copy-start.5
  302.3 0.0 copy-start.7
  302.4 6.8 %fusion.1 = bf16[1,224,7168]{2,1,0:T(8,128)(2,1)} fusion(bf16[512,224]{0,1:T(8,128)(2,1)S(1)} %get-tuple-element.7, bf16[512,7168]{1,0:T(8,128)(2,1)} %reshape.65), kind=kOutput, calls=%fused_computation.7 | convolution fusion | flops 1645772800 | bytes 10780672 | tf_op jit(solution)/shard_map/dot_general | solution.py:16
  309.1 0.0 slice-done
  309.1 0.0 slice-done.1
  309.1 0.0 copy-done.5
  309.1 0.0 copy-done.7
  309.1 3.8 fusion.2
  312.9 0.1 reshape.74
  313.0 0.8 fusion.16
  313.8 170.0 %all-to-all-done.3 = f32[128,4,7168]{2,1,0:T(4,128)} async-done(((f32[128,4,7168]{2,1,0:T(4,128)}), f32[128,4,7168]{2,1,0:T(4,128)}, u32[]{:S(2)}, u32[]{:S(2)}) %all-to-all-start.3) | async-done | bytes 14680096 | tf_op jit(solution)/shard_map/all_to_all | solution.py:90
  483.8 0.0 copy-start.1
  483.8 10.4 %bitcast_reduce_fusion = f32[16,4,7168]{2,1,0:T(4,128)} fusion(f32[128,4,7168]{2,1,0:T(4,128)} %all-to-all-done.3), kind=kLoop, calls=%fused_computation | loop fusion | flops 3211264 | bytes 16515072 | tf_op jit(solution)/shard_map/reduce_sum | solution.py:105
  494.1 2.9 reshape.68
  497.0 5.8 %convolution_convert_fusion.3 = bf16[128,7168]{1,0:T(8,128)(2,1)} fusion(f32[128,64]{0,1:T(8,128)S(1)} %convert_reduce_fusion, f32[64,7168]{1,0:T(8,128)} %reshape.68), kind=kOutput, calls=%fused_computation.9 | convolution fusion | flops 705560576 | bytes 3702784 | tf_op jit(solution)/shard_map/dot_general | solution.py:107
  502.9 0.0 copy-done.1
  (3 shorter events, 0.1 us)
Async XLA Ops:
  0.6 245.1 %copy-start = (bf16[1,224,7168]{2,1,0:T(8,128)(2,1)S(1)}, bf16[1,224,7168]{2,1,0:T(8,128)(2,1)}, u32[]{:S(2)}) copy-start(bf16[1,224,7168]{2,1,0:T(8,128)(2,1)} %param.14) | copy-start | bytes 9633796
  3.6 21.3 %all-to-all-start = ((bf16[128,1,4]{2,1,0:T(2,128)(2,1)}), bf16[128,1,4]{2,1,0:T(2,128)(2,1)S(1)}, u32[]{:S(2)}, u32[]{:S(2)}) async-start(bf16[128,1,4]{2,1,0:T(2,128)(2,1)} %copy.22), calls=%async_computation | async-start | bytes 131072 | tf_op jit(solution)/shard_map/all_to_all | solution.py:75
  31.3 93.7 %all-to-all-start.1 = ((bf16[128,4,7168]{2,1,0:T(4,128)(2,1)}), bf16[128,4,7168]{2,1,0:T(4,128)(2,1)}, u32[]{:S(2)}, u32[]{:S(2)}) async-start(bf16[128,4,7168]{2,1,0:T(4,128)(2,1)} %bitcast.54), calls=%async_computation.1 | async-start | bytes 14680064 | tf_op jit(solution)/shard_map/all_to_all | solution.py:74
  131.3 95.8 %all-to-all-start.2 = ((bf16[128,4,7168]{2,1,0:T(4,128)(2,1)}), bf16[128,4,7168]{2,1,0:T(4,128)(2,1)}, u32[]{:S(2)}, u32[]{:S(2)}) async-start(bf16[128,4,7168]{2,1,0:T(4,128)(2,1)} %bitcast.53), calls=%async_computation.2 | async-start | bytes 14680064 | tf_op jit(solution)/shard_map/all_to_all | solution.py:73
  239.2 6.5 %copy-start.2 = (bf16[512,7168]{1,0:T(8,128)(2,1)S(1)}, bf16[512,7168]{1,0:T(8,128)(2,1)}, u32[]{:S(2)}) copy-start(bf16[512,7168]{1,0:T(8,128)(2,1)} %reshape.65) | copy-start | bytes 22020100
  239.2 6.5 %copy-start.6 = (f32[512,224]{0,1:T(8,128)S(1)}, f32[512,224]{0,1:T(8,128)}, u32[]{:S(2)}) copy-start(f32[512,224]{0,1:T(8,128)} %fusion.11) | copy-start | bytes 1376260
  245.8 3.3 copy-start.4
  249.8 35.6 %all-to-all-start.4 = ((f32[128,1,4]{2,1,0:T(1,128)}), f32[128,1,4]{2,1,0:T(1,128)S(1)}, u32[]{:S(2)}, u32[]{:S(2)}) async-start(f32[128,1,4]{2,1,0:T(1,128)} %bitcast.58), calls=%async_computation.4 | async-start | bytes 131072 | tf_op jit(solution)/shard_map/all_to_all | solution.py:97
  285.4 10.2 %copy-start.3 = (bf16[512,224]{0,1:T(8,128)(2,1)S(1)}, bf16[512,224]{0,1:T(8,128)(2,1)}, u32[]{:S(2)}) copy-start(bf16[512,224]{0,1:T(8,128)(2,1)} %get-tuple-element.6) | copy-start | bytes 688132
  285.4 198.4 %all-to-all-start.3 = ((f32[128,4,7168]{2,1,0:T(4,128)}), f32[128,4,7168]{2,1,0:T(4,128)}, u32[]{:S(2)}, u32[]{:S(2)}) async-start(f32[128,4,7168]{2,1,0:T(4,128)} %reshape.66), calls=%async_computation.3 | async-start | bytes 29360128 | tf_op jit(solution)/shard_map/all_to_all | solution.py:90
  295.6 13.5 %slice-start = ((s8[7340032]{0:T(1024)(128)(4,1)}), s8[4194304]{0:T(1024)(128)(4,1)S(1)}, s32[]{:S(2)}) async-start(s8[7340032]{0:T(1024)(128)(4,1)} %bitcast.55), calls=%async_computation.5 | async-start | bytes 8388608
  302.3 6.8 %slice-start.1 = ((s8[7340032]{0:T(1024)(128)(4,1)}), s8[3145728]{0:T(1024)(128)(4,1)S(1)}, s32[]{:S(2)}) async-start(s8[7340032]{0:T(1024)(128)(4,1)} %bitcast.55), calls=%async_computation.6 | async-start | bytes 6291456
  302.3 6.8 %copy-start.5 = (f32[512,224]{0,1:T(8,128)S(1)}, f32[512,224]{0,1:T(8,128)}, u32[]{:S(2)}) copy-start(f32[512,224]{0,1:T(8,128)} %copy-done.4) | copy-start | bytes 1376260
  302.3 6.8 %copy-start.7 = (f32[512,224]{0,1:T(8,128)S(1)}, f32[512,224]{0,1:T(8,128)}, u32[]{:S(2)}) copy-start(f32[512,224]{0,1:T(8,128)} %get-tuple-element.8) | copy-start | bytes 1376260
  483.8 19.1 %copy-start.1 = (bf16[1,224,7168]{2,1,0:T(8,128)(2,1)S(1)}, bf16[1,224,7168]{2,1,0:T(8,128)(2,1)}, u32[]{:S(2)}) copy-start(bf16[1,224,7168]{2,1,0:T(8,128)(2,1)} %param.14) | copy-start | bytes 9633796
where the time goes:
time: 509 us; the launch traced here: 503 us
  waiting for transfers between devices  326 us (64%)
  local copies, waits for them, and re-layouts  63.9 us (13%)
  matrix products  59 us (12%)
  starting transfers between devices  42.2 us (8%)
  other arithmetic  11.5 us (2%)
    all_to_all x1, waiting for transfers between devices, per_device(): lax.all_to_all(input_part.reshape(copy_shape), ('wide', 'narrow'), split_...  170 us
    all_to_all x1, waiting for transfers between devices, per_device(): lax.all_to_all(fanned_grad, ('wide', 'narrow'), split_axis=0, concat_axis...  82.6 us
    all_to_all x1, waiting for transfers between devices, per_device(): lax.all_to_all(fanned_input, ('wide', 'narrow'), split_axis=0, concat_axi...  68.5 us
    dot_general x5, matrix products, outer_sum(): lax.dot_general(left, right, (((0,), (0,)), ((), ())), preferred_element_...  22.9 us
    reshape x1, local copies, waits for them, and re-layouts, per_device(): input_part.reshape(copy_shape)  17 us
    dot_general x3, matrix products, project(): lax.dot_general(rows, weight, (((1,), (1,)), ((), ())), preferred_element...  16.9 us
    reshape x1, local copies, waits for them, and re-layouts, per_device(): rows_input = recv_input.reshape(-1, model_width)  12.1 us
    reshape x1, local copies, waits for them, and re-layouts, per_device(): recv_grad.reshape(-1, model_width)  12.1 us
  transfers between devices with their start and end apart: 5, of which 4 were waited for; matrix products, arithmetic and copies ran while one was open for 15% of the time, Pallas kernels for 0%

commit v1 on v0

v1 whole, which is shorter than its diff:
```python
import functools

import jax
import jax.numpy as jnp
from jax import lax
from jax.experimental import pallas as pl
from jax.experimental.pallas import tpu as pltpu
from jax.sharding import PartitionSpec as P

CAP = 4
WIDE = 16
NARROW = 8
ROWS = WIDE * CAP
CHUNKS = 8
UNITS = 2 * CHUNKS
PAD = 256
MESH = pl.DeviceIdType.MESH
F32 = jnp.float32
BF16 = jnp.bfloat16


def dot(left, right):
    return jnp.dot(left, right, preferred_element_type=F32)


def dot_nt(left, right):
    return lax.dot_general(left, right, (((1,), (1,)), ((), ())), preferred_element_type=F32)


def iota(shape, dim):
    return lax.broadcasted_iota(jnp.int32, shape, dim)


def gather_is_b(unit):
    stage, quarter = unit // 4, unit % 4
    return ((stage % 2 == 0) & (quarter % 2 == 1)) | ((stage % 2 == 1) & (quarter == 2))


def reduce_is_b(chunk):
    return (chunk % 2 == 1) & (chunk < 6)


def kernel(
    ids_ref,
    slots_ref,
    gates_ref,
    tok_hbm,
    cot_hbm,
    wg_hbm,
    wu_hbm,
    wd_hbm,
    gt_hbm,
    gg_ref,
    og_hbm,
    ou_hbm,
    od_hbm,
    place,
    place_t,
    tokbuf,
    sendbuf,
    a2abuf,
    xbuf,
    wab,
    wdn,
    acc_ab,
    acc_u,
    gsend,
    ga2a,
    gbuf,
    dd,
    dd_t,
    hq_t,
    pbuf,
    rb,
    fin,
    rbuf,
    retsend,
    retbuf,
    stage_ab,
    stage_d,
    gp,
    gpr,
    gsum,
    gret,
    tok_sem,
    w_sem,
    a2a_s,
    a2a_r,
    ga_s,
    ga_r,
    gg_s,
    gg_r,
    ag_s,
    ag_r,
    c_s,
    c_r,
    ret_s,
    ret_r,
    gp_s,
    gp_r,
    gr_s,
    gr_r,
    out_sem,
    gt_sem,
):
    w = lax.axis_index("wide")
    n = lax.axis_index("narrow")
    y, xh = n // 2, n % 2
    yp, ym, y2 = (y + 1) % 4, (y + 3) % 4, (y + 2) % 4
    ox = 1 - xh
    cw = tokbuf.shape[2]
    hid = wg_hbm.shape[1]

    def at(yy, xx):
        return yy * 2 + xx

    dev_p, dev_m, dev_x = at(yp, xh), at(ym, xh), at(y, ox)

    def cols(chunk):
        return pl.ds(pl.multiple_of(chunk * cw, 128), cw)

    def remote(src, dst, ss, rs, to_w, to_n):
        return pltpu.make_async_remote_copy(
            src_ref=src,
            dst_ref=dst,
            send_sem=ss,
            recv_sem=rs,
            device_id=(to_w, to_n),
            device_id_type=MESH,
        )

    barrier = pltpu.get_barrier_semaphore()

    @pl.loop(1, WIDE)
    def _(i):
        pl.semaphore_signal(barrier, inc=1, device_id=((w + i) % WIDE, n), device_id_type=MESH)

    @pl.loop(1, NARROW)
    def _(i):
        pl.semaphore_signal(barrier, inc=1, device_id=(w, (n + i) % NARROW), device_id_type=MESH)

    def tok_copy(half, arr, quarter):
        src = tok_hbm if arr == 0 else cot_hbm
        return pltpu.make_async_copy(
            src.at[:, cols(half * 4 + quarter)],
            tokbuf.at[half * 2 + arr, pl.ds(quarter * 128, 128)],
            tok_sem.at[half * 2 + arr, quarter],
        )

    for half in range(2):
        for arr in range(2):
            for quarter in range(4):
                tok_copy(half, arr, quarter).start()

    def w_copies(chunk):
        return (
            pltpu.make_async_copy(
                wg_hbm.at[0, :, cols(chunk)], wab.at[chunk, pl.ds(0, hid)], w_sem.at[0, chunk]
            ),
            pltpu.make_async_copy(
                wu_hbm.at[0, :, cols(chunk)], wab.at[chunk, pl.ds(PAD, hid)], w_sem.at[1, chunk]
            ),
            pltpu.make_async_copy(
                wd_hbm.at[0, :, cols(chunk)], wdn.at[chunk, pl.ds(0, hid)], w_sem.at[2, chunk]
            ),
        )

    kept = (ids_ref[...] < WIDE) & (slots_ref[...] < CAP)
    target = jnp.where(kept, ids_ref[...] * CAP + slots_ref[...], ROWS)
    row = iota((256, 128), 0)
    code = (row >> 4) * CAP + (row & 3)
    hit = jnp.zeros((256, 128), F32)
    weight = jnp.zeros((256, 128), F32)
    for k in range(8):
        match = target[k : k + 1, :] == code
        hit = hit + jnp.where(match, 1.0, 0.0)
        weight = weight + jnp.where(match, gates_ref[k : k + 1, :], 0.0)
    for q in range(4):
        part = jnp.where(((row >> 2) & 3) == q, hit, 0.0)
        place[:, q * 128 : (q + 1) * 128] = part.astype(BF16)
        place_t[q * 128 : (q + 1) * 128, :] = part.T.astype(BF16)
    gsend[...] = (
        dot(weight.astype(BF16), jnp.ones((128, 128), BF16)).astype(BF16).reshape(WIDE, 16, 128)
    )

    pl.semaphore_wait(barrier, WIDE + NARROW - 2)

    def a2a_copy(st, i):
        e = (w + i) % WIDE
        return remote(
            sendbuf.at[st, e], a2abuf.at[st, w], a2a_s.at[st, i], a2a_r.at[st, i], e, n
        )

    def ga_copy(i):
        e = (w + i) % WIDE
        return remote(gsend.at[e], ga2a.at[w], ga_s.at[i], ga_r.at[i], e, n)

    def pack(st, half, arr):
        for quarter in range(4):
            tok_copy(half, arr, quarter).wait()
        block = dot(place[...], tokbuf[st]).astype(BF16).reshape(WIDE, 16, cw)
        sendbuf[st] = block

        @pl.loop(1, WIDE)
        def _(i):
            a2a_copy(st, i).start()

        a2abuf[st, w] = sendbuf[st, w]

    for half in range(2):
        for arr in range(2):
            pack(half * 2 + arr, half, arr)
            if half == 0 and arr == 0:

                @pl.loop(1, WIDE)
                def _(i):
                    ga_copy(i).start()

                ga2a[w] = gsend[w]

                @pl.loop(0, CHUNKS)
                def _(chunk):
                    for cp in w_copies(chunk):
                        cp.start()
                    wab[chunk, hid:PAD] = jnp.zeros((PAD - hid, cw), BF16)
                    wab[chunk, PAD + hid :] = jnp.zeros((PAD - hid, cw), BF16)
                    wdn[chunk, hid:] = jnp.zeros((PAD - hid, cw), BF16)

    acc_ab[...] = jnp.zeros_like(acc_ab)
    acc_u[...] = jnp.zeros_like(acc_u)

    r2, c2 = iota((256, 256), 0), iota((256, 256), 1)
    sort_rows = (
        ((r2 >> 6) == ((c2 >> 2) & 3)) & (((r2 >> 2) & 15) == (c2 >> 4)) & ((r2 & 3) == (c2 & 3))
    )
    sort_rows = jnp.where(sort_rows, 1.0, 0.0).astype(BF16)
    unsort_rows = (
        ((c2 >> 6) == ((r2 >> 2) & 3)) & (((c2 >> 2) & 15) == (r2 >> 4)) & ((c2 & 3) == (r2 & 3))
    )
    unsort_rows = jnp.where(unsort_rows, 1.0, 0.0).astype(BF16)

    def ag_copy(u, s, piece, to_n):
        return remote(xbuf.at[u, piece], xbuf.at[u, piece], ag_s.at[u, s], ag_r.at[u, piece], w, to_n)

    def ag_half(u, s, piece, lower, sem, to_n):
        ref = xbuf.at[u, piece, pl.ds(0 if lower else 32, 32)]
        return remote(ref, ref, ag_s.at[u, s], ag_r.at[u, sem], w, to_n)

    def sends_a(u):
        return (
            (
                part(ag_copy, u, 0, n, dev_x),
                part(ag_copy, u, 1, n, dev_p),
                part(ag_copy, u, 2, n, dev_m),
            ),
            (part(ag_copy, u, 3, dev_x, dev_p), part(ag_copy, u, 4, dev_x, dev_m)),
            (part(ag_copy, u, 5, dev_m, dev_p), part(ag_copy, u, 6, at(yp, ox), dev_m)),
        )

    def sends_b(u):
        return (
            (
                part(ag_copy, u, 0, n, dev_p),
                part(ag_copy, u, 1, n, dev_m),
                part(ag_copy, u, 2, n, dev_x),
            ),
            (
                part(ag_half, u, 3, dev_m, True, dev_m, dev_p),
                part(ag_half, u, 4, dev_p, False, NARROW, dev_m),
                part(ag_copy, u, 5, dev_m, dev_x),
                part(ag_copy, u, 6, dev_p, dev_x),
            ),
            (part(ag_copy, u, 7, at(y2, xh), dev_x),),
        )

    def arrive(u, piece):
        ag_copy(u, 0, piece, dev_x).wait_recv()

    part = functools.partial

    def start_all(copies):
        for cp in copies:
            cp().start()

    def sort_stage(st):
        @pl.loop(1, WIDE)
        def _(i):
            src = (w + WIDE - i) % WIDE
            remote(
                a2abuf.at[st, src], a2abuf.at[st, src], a2a_s.at[st, i], a2a_r.at[st, i], src, n
            ).wait_recv()

        rows = dot(sort_rows, a2abuf[st].reshape(256, cw)).astype(BF16)
        for q in range(4):
            xbuf[st * 4 + q, n] = rows[q * ROWS : (q + 1) * ROWS]

    def gg_copy(i):
        return remote(gbuf.at[n], gbuf.at[n], gg_s.at[i], gg_r.at[i], w, (n + i) % NARROW)

    @pl.loop(0, UNITS + 3)
    def _(t):
        @pl.when(t < UNITS)
        def _():
            @pl.when(t % 4 == 0)
            def _():
                sort_stage(t // 4)

            @pl.when(gather_is_b(t))
            def _():
                start_all(sends_b(t)[0])

            @pl.when(jnp.logical_not(gather_is_b(t)))
            def _():
                start_all(sends_a(t)[0])

            @pl.when(t == 2)
            def _():
                @pl.loop(1, WIDE)
                def _(i):
                    src = (w + WIDE - i) % WIDE
                    remote(
                        ga2a.at[src], ga2a.at[src], ga_s.at[i], ga_r.at[i], src, n
                    ).wait_recv()

                gbuf[n] = dot(sort_rows[0:ROWS], ga2a[...].reshape(256, 128)).astype(BF16)

                @pl.loop(1, NARROW)
                def _(i):
                    gg_copy(i).start()

        u1 = t - 1

        @pl.when((u1 >= 0) & (u1 < UNITS))
        def _():
            @pl.when(gather_is_b(u1))
            def _():
                arrive(u1, dev_m)
                arrive(u1, dev_p)
                start_all(sends_b(u1)[1])

            @pl.when(jnp.logical_not(gather_is_b(u1)))
            def _():
                arrive(u1, dev_x)
                start_all(sends_a(u1)[1])

        u2 = t - 2

        @pl.when((u2 >= 0) & (u2 < UNITS))
        def _():
            @pl.when(gather_is_b(u2))
            def _():
                ag_half(u2, 0, at(y2, xh), True, at(y2, xh), dev_x).wait_recv()
                ag_half(u2, 0, at(y2, xh), False, NARROW, dev_x).wait_recv()
                start_all(sends_b(u2)[2])

            @pl.when(jnp.logical_not(gather_is_b(u2)))
            def _():
                for yy in (ym, yp):
                    arrive(u2, at(yy, xh))
                    arrive(u2, at(yy, ox))
                start_all(sends_a(u2)[2])

        u3 = t - 3

        @pl.when(u3 >= 0)
        def _():
            @pl.when(gather_is_b(u3))
            def _():
                for yy in (y, yp, ym, y2):
                    arrive(u3, at(yy, ox))

            @pl.when(jnp.logical_not(gather_is_b(u3)))
            def _():
                arrive(u3, at(y2, xh))
                arrive(u3, at(y2, ox))

            chunk = (u3 // 8) * 4 + u3 % 4
            is_cot = (u3 // 4) % 2 == 1
            rows = xbuf.at[u3]

            @pl.when(is_cot)
            def _():
                w_copies(chunk)[2].wait()
                acc_u[...] += dot_nt(rows[...].reshape(512, cw), wdn[chunk])

            @pl.when(jnp.logical_not(is_cot))
            def _():
                w_copies(chunk)[0].wait()
                w_copies(chunk)[1].wait()
                acc_ab[...] += dot_nt(rows[...].reshape(512, cw), wab[chunk])

    @pl.loop(1, NARROW)
    def _(i):
        src = (n + NARROW - i) % NARROW
        remote(gbuf.at[src], gbuf.at[src], gg_s.at[i], gg_r.at[i], w, src).wait_recv()

    gp[4:8] = jnp.zeros((4, 128), F32)
    for r in range(4):
        span = slice(r * 128, (r + 1) * 128)
        g = gbuf[2 * r : 2 * r + 2].reshape(128, 128).astype(F32)
        g = jnp.concatenate([g, g], axis=1)
        a = acc_ab[span, 0:PAD]
        b = acc_ab[span, PAD : 2 * PAD]
        u = acc_u[span, :]
        s = jax.nn.sigmoid(a)
        act = a * s
        dh = g * u
        da = dh * b * s * (1.0 + a * (1.0 - s))
        du = dh * act
        h = act * b
        dd[span, 0:PAD] = da.astype(BF16)
        dd[span, PAD : 2 * PAD] = du.astype(BF16)
        dd_t[0:PAD, span] = da.T.astype(BF16)
        dd_t[PAD : 2 * PAD, span] = du.T.astype(BF16)
        hq_t[:, span] = h.T.astype(BF16)
        gp[r : r + 1, :] = jnp.sum((u * h).T, axis=0, keepdims=True)

    def gp_copy(i):
        return remote(gp, gpr.at[n], gp_s.at[i], gp_r.at[i], w, (n + i) % NARROW)

    def gr_copy(i):
        e = (w + i) % WIDE
        return remote(gsum, gret.at[w], gr_s.at[i], gr_r.at[i], e, n)

    gpr[n] = gp[...]

    @pl.loop(1, NARROW)
    def _(i):
        gp_copy(i).start()

    lo, hi = pl.ds(0, 32), pl.ds(32, 32)

    def c_copy(k, s, piece, slot, to_n):
        return remote(pbuf.at[k, piece], rb.at[k, slot], c_s.at[k, s], c_r.at[k, s], w, to_n)

    def c_half(k, s, piece, slot, span, to_n):
        return remote(
            pbuf.at[k, piece, span], rb.at[k, slot, span], c_s.at[k, s], c_r.at[k, s], w, to_n
        )

    def add_into(k, piece, slot, span=slice(None)):
        pbuf[k, piece, span] = (
            pbuf[k, piece, span].astype(F32) + rb[k, slot, span].astype(F32)
        ).astype(BF16)

    def red_a(k):
        return (
            (
                part(c_copy, k, 0, at(y2, 0), 0, dev_p),
                part(c_copy, k, 1, at(y2, 1), 1, dev_m),
                part(c_copy, k, 3, at(yp, 1), 3, dev_p),
                part(c_copy, k, 4, at(ym, 0), 4, dev_m),
            ),
            (part(c_copy, k, 2, at(yp, 0), 2, dev_p), part(c_copy, k, 5, at(ym, 1), 5, dev_m)),
            (part(c_copy, k, 6, at(y, ox), 6, dev_x),),
        )

    def red_b(k):
        return (
            tuple(part(c_copy, k, yy, at(yy, ox), yy, dev_x) for yy in range(4)),
            (
                part(c_half, k, 4, at(y2, xh), 4, lo, dev_p),
                part(c_half, k, 5, at(y2, xh), 4, hi, dev_m),
                part(c_half, k, 7, at(yp, xh), 5, hi, dev_p),
                part(c_half, k, 8, at(ym, xh), 6, lo, dev_m),
            ),
            (
                part(c_half, k, 6, at(yp, xh), 5, lo, dev_p),
                part(c_half, k, 9, at(ym, xh), 6, hi, dev_m),
            ),
        )

    def ret_copy(h, i):
        to = (w + i) % WIDE
        return remote(
            retsend.at[h, to], retbuf.at[h, w], ret_s.at[h, i], ret_r.at[h, i], to, n
        )

    def out_copies(k, slot):
        return (
            pltpu.make_async_copy(
                stage_ab.at[slot, pl.ds(0, hid)], og_hbm.at[0, :, cols(k)], out_sem.at[slot, 0]
            ),
            pltpu.make_async_copy(
                stage_ab.at[slot, pl.ds(PAD, hid)], ou_hbm.at[0, :, cols(k)], out_sem.at[slot, 1]
            ),
            pltpu.make_async_copy(
                stage_d.at[slot, pl.ds(0, hid)], od_hbm.at[0, :, cols(k)], out_sem.at[slot, 2]
            ),
        )

    @pl.loop(0, CHUNKS + 3)
    def _(t):
        @pl.when(t < CHUNKS)
        def _():
            pbuf[t] = dot(dd[...], wab[t]).astype(BF16).reshape(NARROW, ROWS, cw)

            @pl.when(reduce_is_b(t))
            def _():
                start_all(red_b(t)[0])

            @pl.when(jnp.logical_not(reduce_is_b(t)))
            def _():
                start_all(red_a(t)[0])

        k1 = t - 1

        @pl.when((k1 >= 0) & (k1 < CHUNKS))
        def _():
            @pl.when(reduce_is_b(k1))
            def _():
                for cp in red_b(k1)[0]:
                    cp().wait_recv()
                fin[k1] = pbuf[k1, n].astype(F32) + rb[k1, y].astype(F32)
                for yy in (y2, yp, ym):
                    add_into(k1, at(yy, xh), yy)
                start_all(red_b(k1)[1])

            @pl.when(jnp.logical_not(reduce_is_b(k1)))
            def _():
                red_a(k1)[0][0]().wait_recv()
                add_into(k1, at(yp, 0), 0)
                red_a(k1)[1][0]().start()
                red_a(k1)[0][1]().wait_recv()
                add_into(k1, at(ym, 1), 1)
                red_a(k1)[1][1]().start()

        k2 = t - 2

        @pl.when((k2 >= 0) & (k2 < CHUNKS))
        def _():
            @pl.when(reduce_is_b(k2))
            def _():
                red_b(k2)[1][0]().wait_recv()
                add_into(k2, at(yp, xh), 4, lo)
                red_b(k2)[2][0]().start()
                red_b(k2)[1][1]().wait_recv()
                add_into(k2, at(ym, xh), 4, hi)
                red_b(k2)[2][1]().start()

            @pl.when(jnp.logical_not(reduce_is_b(k2)))
            def _():
                for cp in red_a(k2)[0][2:] + red_a(k2)[1]:
                    cp().wait_recv()
                fin[k2] = (
                    pbuf[k2, n].astype(F32)
                    + rb[k2, 2 + xh].astype(F32)
                    + rb[k2, 4 + xh].astype(F32)
                )
                other = at(y, ox)
                pbuf[k2, other] = (
                    pbuf[k2, other].astype(F32)
                    + rb[k2, 2 + ox].astype(F32)
                    + rb[k2, 4 + ox].astype(F32)
                ).astype(BF16)
                start_all(red_a(k2)[2])

        k3 = t - 3

        @pl.when(k3 >= 0)
        def _():
            @pl.when(reduce_is_b(k3))
            def _():
                for cp in red_b(k3)[1][2:] + red_b(k3)[2]:
                    cp().wait_recv()
                rbuf[k3] = (
                    fin[k3] + rb[k3, 5].astype(F32) + rb[k3, 6].astype(F32)
                ).astype(BF16)

            @pl.when(jnp.logical_not(reduce_is_b(k3)))
            def _():
                red_a(k3)[2][0]().wait_recv()
                rbuf[k3] = (fin[k3] + rb[k3, 6].astype(F32)).astype(BF16)

            @pl.when(k3 % 4 == 3)
            def _():
                h = k3 // 4
                rows = rbuf[pl.ds(h * 4, 4)].reshape(256, cw)
                retsend[h] = dot(unsort_rows, rows).astype(BF16).reshape(WIDE, 16, cw)

                @pl.loop(1, WIDE)
                def _(i):
                    ret_copy(h, i).start()

                retbuf[h, w] = retsend[h, w]

        @pl.when(t == 3)
        def _():
            @pl.loop(1, NARROW)
            def _(i):
                src = (n + NARROW - i) % NARROW
                remote(gpr.at[src], gpr.at[src], gp_s.at[i], gp_r.at[i], w, src).wait_recv()

            gsum[...] = jnp.sum(gpr[...], axis=0)
            gret[w] = gsum[...]

            @pl.loop(1, WIDE)
            def _(i):
                gr_copy(i).start()

        @pl.when(t < CHUNKS)
        def _():
            slot = t % 2

            @pl.when(t >= 2)
            def _():
                for cp in out_copies(t - 2, slot):
                    cp.wait()

            unit = (t // 4) * 8 + t % 4
            stage_ab[slot] = dot(dd_t[...], xbuf[unit].reshape(512, cw)).astype(BF16)

            @pl.loop(0, NARROW)
            def _(piece):
                g = gbuf[piece].astype(F32)
                g = jnp.concatenate([g] * (cw // 128), axis=1)
                tokbuf[2, pl.ds(piece * ROWS, ROWS)] = (
                    g * xbuf[unit + 4, piece].astype(F32)
                ).astype(BF16)

            stage_d[slot] = dot(hq_t[...], tokbuf[2]).astype(BF16)
            for cp in out_copies(t, slot):
                cp.start()

    @pl.loop(1, WIDE)
    def _(i):
        src = (w + WIDE - i) % WIDE
        remote(gret.at[src], gret.at[src], gr_s.at[i], gr_r.at[i], src, n).wait_recv()

    row64 = iota((ROWS, WIDE), 0)
    spread = jnp.where((row64 >> 2) == iota((ROWS, WIDE), 1), 1.0, 0.0)
    line = gret[:, n // 2, :]
    table = lax.dot_general(
        spread,
        line,
        (((1,), (0,)), ((), ())),
        precision=lax.Precision.HIGHEST,
        preferred_element_type=F32,
    )
    slot_row = iota((ROWS, 128), 0)
    lane = (n % 2) * 64 + w * CAP + (slot_row & 3)
    column = jnp.sum(
        jnp.where(iota((ROWS, 128), 1) == lane, table, 0.0), axis=1, keepdims=True
    )
    for k in range(8):
        match = target[k : k + 1, :] == slot_row
        gg_ref[k : k + 1, :] = jnp.sum(jnp.where(match, column, 0.0), axis=0, keepdims=True)

    def gt_copy(h, q):
        return pltpu.make_async_copy(
            tokbuf.at[h, pl.ds(q * 128, 128)], gt_hbm.at[:, cols(h * 4 + q)], gt_sem.at[h, q]
        )

    for h in range(2):

        @pl.loop(1, WIDE)
        def _(i):
            src = (w + WIDE - i) % WIDE
            remote(
                retbuf.at[h, src], retbuf.at[h, src], ret_s.at[h, i], ret_r.at[h, i], src, n
            ).wait_recv()

        tokbuf[h] = dot(place_t[...], retbuf[h].reshape(256, cw)).astype(BF16)
        for q in range(4):
            gt_copy(h, q).start()

    @pl.loop(1, WIDE)
    def _(i):
        for st in range(4):
            a2a_copy(st, i).wait_send()
        ga_copy(i).wait_send()
        gr_copy(i).wait_send()
        for h in range(2):
            ret_copy(h, i).wait_send()

    @pl.loop(1, NARROW)
    def _(i):
        gg_copy(i).wait_send()
        gp_copy(i).wait_send()

    @pl.loop(0, UNITS)
    def _(u):
        @pl.when(gather_is_b(u))
        def _():
            for group in sends_b(u):
                for cp in group:
                    cp().wait_send()

        @pl.when(jnp.logical_not(gather_is_b(u)))
        def _():
            for group in sends_a(u):
                for cp in group:
                    cp().wait_send()

    @pl.loop(0, CHUNKS)
    def _(k):
        @pl.when(reduce_is_b(k))
        def _():
            for group in red_b(k):
                for cp in group:
                    cp().wait_send()

        @pl.when(jnp.logical_not(reduce_is_b(k)))
        def _():
            for group in red_a(k):
                for cp in group:
                    cp().wait_send()

    for k in (CHUNKS - 2, CHUNKS - 1):
        for cp in out_copies(k, k % 2):
            cp.wait()
    for h in range(2):
        for q in range(4):
            gt_copy(h, q).wait()


def per_device(tokens, grad_out, gates, expert_ids, slots, w_gate, w_up, w_down):
    width = tokens.shape[1]
    cw = width // CHUNKS
    any_spec = pl.BlockSpec(memory_space=pl.ANY)
    vmem_spec = pl.BlockSpec(memory_space=pltpu.VMEM)
    vm = pltpu.VMEM
    dma = pltpu.SemaphoreType.DMA
    gt, gg, og, ou, od = pl.pallas_call(
        kernel,
        out_shape=(
            jax.ShapeDtypeStruct(tokens.shape, BF16),
            jax.ShapeDtypeStruct((8, 128), F32),
            jax.ShapeDtypeStruct(w_gate.shape, BF16),
            jax.ShapeDtypeStruct(w_up.shape, BF16),
            jax.ShapeDtypeStruct(w_down.shape, BF16),
        ),
        in_specs=[vmem_spec] * 3 + [any_spec] * 5,
        out_specs=(any_spec, vmem_spec, any_spec, any_spec, any_spec),
        scratch_shapes=[
            vm((256, 512), BF16),
            vm((512, 256), BF16),
            vm((4, 512, cw), BF16),
            vm((4, WIDE, 16, cw), BF16),
            vm((4, WIDE, 16, cw), BF16),
            vm((UNITS, NARROW, ROWS, cw), BF16),
            vm((CHUNKS, 2 * PAD, cw), BF16),
            vm((CHUNKS, PAD, cw), BF16),
            vm((512, 2 * PAD), F32),
            vm((512, PAD), F32),
            vm((WIDE, 16, 128), BF16),
            vm((WIDE, 16, 128), BF16),
            vm((NARROW, ROWS, 128), BF16),
            vm((512, 2 * PAD), BF16),
            vm((2 * PAD, 512), BF16),
            vm((PAD, 512), BF16),
            vm((CHUNKS, NARROW, ROWS, cw), BF16),
            vm((CHUNKS, 7, ROWS, cw), BF16),
            vm((CHUNKS, ROWS, cw), F32),
            vm((CHUNKS, ROWS, cw), BF16),
            vm((2, WIDE, 16, cw), BF16),
            vm((2, WIDE, 16, cw), BF16),
            vm((2, 2 * PAD, cw), BF16),
            vm((2, PAD, cw), BF16),
            vm((8, 128), F32),
            vm((NARROW, 8, 128), F32),
            vm((8, 128), F32),
            vm((WIDE, 8, 128), F32),
            dma((4, 4)),
            dma((3, CHUNKS)),
            dma((4, WIDE)),
            dma((4, WIDE)),
            dma((WIDE,)),
            dma((WIDE,)),
            dma((NARROW,)),
            dma((NARROW,)),
            dma((UNITS, 8)),
            dma((UNITS, NARROW + 1)),
            dma((CHUNKS, 10)),
            dma((CHUNKS, 10)),
            dma((2, WIDE)),
            dma((2, WIDE)),
            dma((NARROW,)),
            dma((NARROW,)),
            dma((WIDE,)),
            dma((WIDE,)),
            dma((2, 3)),
            dma((2, 4)),
        ],
        compiler_params=pltpu.CompilerParams(
            collective_id=0, has_side_effects=True, vmem_limit_bytes=63 * 2**20
        ),
        name="routed_backward",
    )(
        expert_ids.T,
        slots.T,
        gates.T.astype(F32),
        tokens,
        grad_out,
        w_gate,
        w_up,
        w_down,
    )
    return (gt, gg.T, og, ou, od)


def solution(mesh):
    rows = P(("wide", "narrow"), None)
    weights = P("wide", "narrow", None)
    return jax.shard_map(
        per_device,
        mesh=mesh,
        in_specs=(rows,) * 5 + (weights,) * 3,
        out_specs=(rows, rows, weights, weights, weights),
        check_vma=False,
    )
```

time: 509 us -> 220 us (0.43); the launches traced: 503 us -> 219 us
  waiting for transfers between devices: 326 us -> 0 us
  Pallas kernels: 0 us -> 206 us
  matrix products: 59 us -> 0 us
  local copies, waits for them, and re-layouts: 63.9 us -> 11.4 us
  starting transfers between devices: 42.2 us -> 0 us
  other arithmetic: 11.5 us -> 1.28 us
    all_to_all x5 -> x0, waiting for transfers between devices: 326 us -> none  [the longest x1 170 us: per_device(): lax.all_to_all(input_part.reshape(copy_shape), ('wide', 'narrow'), split_...]
    pallas_call x0 -> x1, Pallas kernels: none -> 206 us  [per_device(): pl.pallas_call(kernel, out_shape=(jax.ShapeDtypeStruct(tokens.shape, BF16...]
    dot_general x13 -> x0, matrix products: 59 us -> none  [the longest x5 22.9 us: outer_sum(): lax.dot_general(left, right, (((0,), (0,)), ((), ())), preferred_element_...]
    reshape x5 -> x0, local copies, waits for them, and re-layouts: 44.2 us -> none  [the longest x1 17 us: per_device(): input_part.reshape(copy_shape)]
    all_to_all x5 -> x0, starting transfers between devices: 42.2 us -> none  [the longest x1 11.5 us: per_device(): lax.all_to_all(fanned_weight, ('wide', 'narrow'), split_axis=0, concat_ax...]
    broadcast_in_dim x7 -> x0, local copies, waits for them, and re-layouts: 17.9 us -> none  [the longest x2 8.88 us: per_device(): jnp.broadcast_to(send_grad[:, None], (n_wide, n_narrow, CAP, model_width))]
    unnamed x20 -> x13, local copies, waits for them, and re-layouts: 0.05 us -> 11.4 us
    reduce_sum x3 -> x0, other arithmetic: 10.4 us -> none  [the longest x1 10.4 us: per_device(): jnp.sum(back_input.reshape(n_wide, n_narrow, CAP, model_width), axis=1)]
  transfers between devices with their start and end apart: 5 -> 0, of which waited for: 4 -> 0; matrix products, arithmetic and copies ran while one was open for 15% -> 0% of each run, Pallas kernels for 0% -> 0%
where the time goes in v1:
time: 220 us; the launch traced here: 219 us
  Pallas kernels  206 us (94%)
  local copies, waits for them, and re-layouts  11.4 us (5%)
    pallas_call x1, Pallas kernels, per_device(): pl.pallas_call(kernel, out_shape=(jax.ShapeDtypeStruct(tokens.shape, BF16...  206 us
    unnamed x13, local copies, waits for them, and re-layouts  11.4 us

profile of v1, /device:TPU:1, one launch (start us, length us, event | category | flops | bytes accessed | tf_op | source)
XLA Modules:
  0.0 219.3 jit_solution(2483598840509915629)
XLA Ops:
  0.6 1.3 convert_bitcast_fusion.gates_ref
  1.9 205.9 %routed_backward.1 = (bf16[128,7168]{1,0:T(8,128)(2,1)}, f32[8,128]{1,0:T(8,128)}, bf16[1,224,7168]{2,1,0:T(8,128)(2,1)}, bf16[1,224,7168]{2,1,0:T(8,128)(2,1)}, bf16[1,224,7168]{2,1,0:T(8,128)(2,1)}) custom-call(s32[8,128]{1,0:T(8,128)} %bitcast.5, s32[8,128]{1,0:T(8,128)} %bitcast.6, f32[8,128]{1,0:T(8,128)} %convert_bitcast_fusion.gates_ref, ...), custom_call_target="tpu_custom_call" | custom-call | tf_op jit(solution)/shard_map/routed_backward/pallas_call | solution.py:724
  207.8 0.0 copy-start.3
  207.9 0.0 copy-start.2
  207.9 3.0 %copy.18 = bf16[128,7168]{1,0:T(8,128)(2,1)} copy(bf16[128,7168]{1,0:T(8,128)(2,1)} %get-tuple-element.20) | data formatting | bytes 3670016
  210.9 0.0 copy-done.3
  210.9 0.6 copy.19
  211.5 0.0 copy-done.2
  211.5 0.0 copy-start.1
  211.5 1.7 copy.20
  213.1 1.4 copy-done.1
  214.5 0.0 copy-start
  214.5 1.7 copy.21
  216.2 1.4 copy-done
  217.6 1.7 copy.22
Async XLA Ops:
  207.8 3.0 %copy-start.3 = (f32[8,128]{1,0:T(8,128)S(1)}, f32[8,128]{1,0:T(8,128)}, u32[]{:S(2)}) copy-start(f32[8,128]{1,0:T(8,128)} %get-tuple-element.11) | copy-start | bytes 12292
  207.9 3.6 %copy-start.2 = (bf16[1,224,7168]{2,1,0:T(8,128)(2,1)S(1)}, bf16[1,224,7168]{2,1,0:T(8,128)(2,1)}, u32[]{:S(2)}) copy-start(bf16[1,224,7168]{2,1,0:T(8,128)(2,1)} %get-tuple-element.22) | copy-start | bytes 9633796
  211.5 3.1 %copy-start.1 = (bf16[1,224,7168]{2,1,0:T(8,128)(2,1)S(1)}, bf16[1,224,7168]{2,1,0:T(8,128)(2,1)}, u32[]{:S(2)}) copy-start(bf16[1,224,7168]{2,1,0:T(8,128)(2,1)} %get-tuple-element.23) | copy-start | bytes 9633796
  214.5 3.1 %copy-start = (bf16[1,224,7168]{2,1,0:T(8,128)(2,1)S(1)}, bf16[1,224,7168]{2,1,0:T(8,128)(2,1)}, u32[]{:S(2)}) copy-start(bf16[1,224,7168]{2,1,0:T(8,128)(2,1)} %get-tuple-element.24) | copy-start | bytes 9633796

commit v2 on v1

v2 whole, which is shorter than its diff:
```python
import functools

import jax
import jax.numpy as jnp
from jax import lax
from jax.experimental import pallas as pl
from jax.experimental.pallas import tpu as pltpu
from jax.sharding import PartitionSpec as P

CAP = 4
WIDE = 16
NARROW = 8
ROWS = WIDE * CAP
STAGES = 7
CHUNKS = 2 * STAGES
UNITS = 2 * CHUNKS
GATHER_LAG = (2, 4, 6)
REDUCE_LAG = (2, 4, 6)
PAD = 256
MESH = pl.DeviceIdType.MESH
F32 = jnp.float32
BF16 = jnp.bfloat16


def dot(left, right):
    return jnp.dot(left, right, preferred_element_type=F32)


def dot_nt(left, right):
    return lax.dot_general(left, right, (((1,), (1,)), ((), ())), preferred_element_type=F32)


def iota(shape, dim):
    return lax.broadcasted_iota(jnp.int32, shape, dim)


def gather_is_b(unit):
    return (unit * 11 + 17) % 28 < 11


def reduce_is_b(chunk):
    return (chunk * 5) % 14 < 5


def kernel(
    ids_ref,
    slots_ref,
    gates_ref,
    tok_hbm,
    cot_hbm,
    wg_hbm,
    wu_hbm,
    wd_hbm,
    xq_hbm,
    ddt_hbm,
    hqt_hbm,
    placet_hbm,
    ret_hbm,
    gg_ref,
    place,
    place_t,
    tokbuf,
    sendbuf,
    a2abuf,
    xbuf,
    wab,
    wdn,
    acc_ab,
    acc_u,
    gsend,
    ga2a,
    gbuf,
    dd,
    dd_t,
    hq_t,
    pbuf,
    rb,
    fin,
    rbuf,
    retsend,
    qbuf,
    gp,
    gpr,
    gsum,
    gret,
    tok_sem,
    w_sem,
    a2a_s,
    a2a_r,
    g_s,
    g_r,
    ag_s,
    ag_r,
    c_s,
    c_r,
    ret_s,
    ret_r,
    x_sem,
    q_sem,
    out_sem,
):
    w = lax.axis_index("wide")
    n = lax.axis_index("narrow")
    y, xh = n // 2, n % 2
    yp, ym, y2 = (y + 1) % 4, (y + 3) % 4, (y + 2) % 4
    ox = 1 - xh
    cw = xbuf.shape[3]
    qw = cw // 2
    sw = 2 * cw
    hid = wg_hbm.shape[1]

    def at(yy, xx):
        return yy * 2 + xx

    xl, core = (w // 2) % 2, w % 2

    def swap(source, expert):
        return (((source // 2) % 2) ^ ((expert // 2) % 2)) & (source % 2)

    dev_p, dev_m, dev_x = at(yp, xh), at(ym, xh), at(y, ox)

    def cols(chunk):
        return pl.ds(pl.multiple_of(chunk * cw, 128), cw)

    def remote(src, dst, ss, rs, to_w, to_n):
        return pltpu.make_async_remote_copy(
            src_ref=src,
            dst_ref=dst,
            send_sem=ss,
            recv_sem=rs,
            device_id=(to_w, to_n),
            device_id_type=MESH,
        )

    barrier = pltpu.get_barrier_semaphore()

    @pl.loop(1, WIDE)
    def _(i):
        pl.semaphore_signal(barrier, inc=1, device_id=((w + i) % WIDE, n), device_id_type=MESH)

    @pl.loop(0, WIDE)
    def _(i):
        pl.semaphore_signal(barrier, inc=1, device_id=(i, at(y, ox)), device_id_type=MESH)

    @pl.loop(1, 4)
    def _(i):
        for xx in range(2):
            pl.semaphore_signal(
                barrier, inc=1, device_id=(w, at((y + i) % 4, xx)), device_id_type=MESH
            )

    def tok_copy(g, arr):
        src = tok_hbm if arr == 0 else cot_hbm
        span = pl.ds(pl.multiple_of(g * sw, 128), sw)
        return pltpu.make_async_copy(src.at[:, span], tokbuf.at[g, arr], tok_sem.at[g])

    @pl.loop(0, STAGES)
    def _(g):
        for arr in range(2):
            tok_copy(g, arr).start()

    def w_copies(chunk):
        return (
            pltpu.make_async_copy(
                wg_hbm.at[0, :, cols(chunk)], wab.at[chunk, pl.ds(0, hid)], w_sem.at[0]
            ),
            pltpu.make_async_copy(
                wu_hbm.at[0, :, cols(chunk)], wab.at[chunk, pl.ds(PAD, hid)], w_sem.at[0]
            ),
            pltpu.make_async_copy(
                wd_hbm.at[0, :, cols(chunk)], wdn.at[chunk, pl.ds(0, hid)], w_sem.at[1]
            ),
        )

    def landed(ref, sem):
        remote(ref, ref, sem, sem, w, n ^ 1).wait_recv()

    def sent(ref, sem):
        remote(ref, ref, sem, sem, w, n ^ 1).wait_send()

    def here(ref, sem):
        pltpu.make_async_copy(ref, ref, sem).wait()

    kept = (ids_ref[...] < WIDE) & (slots_ref[...] < CAP)
    target = jnp.where(kept, ids_ref[...] * CAP + slots_ref[...], ROWS)
    row = iota((256, 128), 0)
    code = (row >> 4) * CAP + (row & 3)
    gates = gates_ref[...].astype(F32)
    hit = jnp.zeros((256, 128), F32)
    weight = jnp.zeros((256, 128), F32)
    for k in range(8):
        match = target[k : k + 1, :] == code
        hit = hit + jnp.where(match, 1.0, 0.0)
        weight = weight + jnp.where(match, gates[k : k + 1, :], 0.0)
    for q in range(4):
        part = jnp.where(((row >> 2) & 3) == q, hit, 0.0)
        place[:, q * 128 : (q + 1) * 128] = part.astype(BF16)
        place_t[q * 128 : (q + 1) * 128, :] = part.T.astype(BF16)
    gsend[...] = (
        dot(weight.astype(BF16), jnp.ones((128, 128), BF16)).astype(BF16).reshape(WIDE, 16, 128)
    )

    pl.semaphore_wait(barrier, 2 * WIDE - 1 + NARROW - 2)

    def a2a_copy(g, i):
        e = (w + i) % WIDE
        return remote(
            sendbuf.at[g, e],
            a2abuf.at[g, w],
            a2a_s.at[g],
            a2a_r.at[g],
            e,
            at(y, xh ^ swap(w, e)),
        )

    def ga_copy(i):
        e = (w + i) % WIDE
        return remote(gsend.at[e], ga2a.at[w], g_s.at[0], g_r.at[0], e, at(y, xh ^ swap(w, e)))

    def pack(g):
        here(tokbuf.at[g], tok_sem.at[g])
        for arr in range(2):
            slab = jnp.concatenate(
                [tokbuf[g, arr, :, q * qw : (q + 1) * qw] for q in range(4)], axis=0
            )
            sendbuf[g, :, arr] = dot(place[...], slab).astype(BF16).reshape(WIDE, 16, qw)

        @pl.loop(1, WIDE)
        def _(i):
            a2a_copy(g, i).start()

        a2abuf[g, w] = sendbuf[g, w]

    pack(0)

    @pl.loop(1, WIDE)
    def _(i):
        ga_copy(i).start()

    ga2a[w] = gsend[w]

    @pl.loop(0, CHUNKS)
    def _(chunk):
        for cp in w_copies(chunk):
            cp.start()
        wab[chunk, hid:PAD] = jnp.zeros((PAD - hid, cw), BF16)
        wab[chunk, PAD + hid :] = jnp.zeros((PAD - hid, cw), BF16)
        wdn[chunk, hid:] = jnp.zeros((PAD - hid, cw), BF16)

    placet_copy = pltpu.make_async_copy(place_t, placet_hbm, out_sem.at[0])
    placet_copy.start()
    acc_ab[...] = jnp.zeros_like(acc_ab)
    acc_u[...] = jnp.zeros_like(acc_u)

    r2, c2 = iota((256, 256), 0), iota((256, 256), 1)
    sort_rows = (
        ((r2 >> 6) == ((c2 >> 2) & 3)) & (((r2 >> 2) & 15) == (c2 >> 4)) & ((r2 & 3) == (c2 & 3))
    )
    sort_rows = jnp.where(sort_rows, 1.0, 0.0).astype(BF16)
    unsort_rows = (
        ((c2 >> 6) == ((r2 >> 2) & 3)) & (((c2 >> 2) & 15) == (r2 >> 4)) & ((c2 & 3) == (r2 & 3))
    )
    unsort_rows = jnp.where(unsort_rows, 1.0, 0.0).astype(BF16)

    def ag_copy(u, s, piece, to_n):
        ref = xbuf.at[u, piece]
        return remote(ref, ref, ag_s.at[u // 7], ag_r.at[u, s], w, to_n)

    def ag_half(u, s, piece, lower, to_n):
        ref = xbuf.at[u, piece, pl.ds(0 if lower else 32, 32)]
        return remote(ref, ref, ag_s.at[u // 7], ag_r.at[u, s], w, to_n)

    part = functools.partial

    def sends_a(u):
        return (
            (
                part(ag_copy, u, 0, n, dev_x),
                part(ag_copy, u, 1, n, dev_p),
                part(ag_copy, u, 1, n, dev_m),
            ),
            (part(ag_copy, u, 1, dev_x, dev_p), part(ag_copy, u, 1, dev_x, dev_m)),
            (part(ag_copy, u, 2, dev_m, dev_p), part(ag_copy, u, 2, at(yp, ox), dev_m)),
        )

    def sends_b(u):
        return (
            (
                part(ag_copy, u, 0, n, dev_p),
                part(ag_copy, u, 0, n, dev_m),
                part(ag_copy, u, 2, n, dev_x),
            ),
            (
                part(ag_half, u, 1, dev_m, True, dev_p),
                part(ag_half, u, 1, dev_p, False, dev_m),
                part(ag_copy, u, 2, dev_m, dev_x),
                part(ag_copy, u, 2, dev_p, dev_x),
            ),
            (part(ag_copy, u, 2, at(y2, xh), dev_x),),
        )

    def start_all(copies):
        for cp in copies:
            cp().start()

    def sort_stage(g):
        landed(a2abuf.at[g, pl.ds(0, WIDE - 1)], a2a_r.at[g])
        for arr in range(2):
            rows = dot(sort_rows, a2abuf[g, :, arr].reshape(256, qw)).astype(BF16)
            for q in range(4):
                xbuf[g * 4 + arr * 2 + q // 2, n, :, (q % 2) * qw : (q % 2 + 1) * qw] = rows[
                    q * ROWS : (q + 1) * ROWS
                ]

    def gg_copy(i):
        return remote(gbuf.at[n], gbuf.at[n], g_s.at[1], g_r.at[1], w, (n + i) % NARROW)

    def x_copy(u):
        return pltpu.make_async_copy(xbuf.at[u], xq_hbm.at[u], x_sem.at[0])

    def q_copy(u):
        return pltpu.make_async_copy(qbuf.at[u % 2], xq_hbm.at[u], q_sem.at[u % 2])

    lag1, lag2, lag3 = GATHER_LAG

    @pl.loop(0, UNITS + lag3)
    def _(t):
        @pl.when(t < UNITS)
        def _():
            @pl.when(t % 4 == 0)
            def _():
                sort_stage(t // 4)

            @pl.when(gather_is_b(t))
            def _():
                start_all(sends_b(t)[0])

            @pl.when(jnp.logical_not(gather_is_b(t)))
            def _():
                start_all(sends_a(t)[0])

        @pl.when(t == 0)
        def _():
            pack(1)

        @pl.when((t % 4 == 1) & (t // 4 + 2 < STAGES))
        def _():
            pack(t // 4 + 2)

        @pl.when(t == 3)
        def _():
            landed(ga2a.at[pl.ds(0, WIDE - 1)], g_r.at[0])
            gbuf[n] = dot(sort_rows[0:ROWS], ga2a[...].reshape(256, 128)).astype(BF16)

            @pl.loop(1, NARROW)
            def _(i):
                gg_copy(i).start()

        @pl.when(t == lag3)
        def _():
            landed(gbuf.at[pl.ds(0, NARROW - 1)], g_r.at[1])
            here(wab.at[:, pl.ds(0, 2 * hid)], w_sem.at[0])
            here(wdn.at[:, pl.ds(0, hid)], w_sem.at[1])

        u1 = t - lag1

        @pl.when((u1 >= 0) & (u1 < UNITS))
        def _():
            @pl.when(gather_is_b(u1))
            def _():
                landed(xbuf.at[u1, pl.ds(0, 2)], ag_r.at[u1, 0])
                start_all(sends_b(u1)[1])

            @pl.when(jnp.logical_not(gather_is_b(u1)))
            def _():
                landed(xbuf.at[u1, 0], ag_r.at[u1, 0])
                start_all(sends_a(u1)[1])

        u2 = t - lag2

        @pl.when((u2 >= 0) & (u2 < UNITS))
        def _():
            @pl.when(gather_is_b(u2))
            def _():
                landed(xbuf.at[u2, 0], ag_r.at[u2, 1])
                start_all(sends_b(u2)[2])

            @pl.when(jnp.logical_not(gather_is_b(u2)))
            def _():
                landed(xbuf.at[u2, pl.ds(0, 4)], ag_r.at[u2, 1])
                start_all(sends_a(u2)[2])

        u3 = t - lag3

        @pl.when(u3 >= 0)
        def _():
            @pl.when(gather_is_b(u3))
            def _():
                landed(xbuf.at[u3, pl.ds(0, 4)], ag_r.at[u3, 2])

            @pl.when(jnp.logical_not(gather_is_b(u3)))
            def _():
                landed(xbuf.at[u3, pl.ds(0, 2)], ag_r.at[u3, 2])

            chunk = (u3 // 4) * 2 + u3 % 2
            is_cot = (u3 // 2) % 2 == 1

            @pl.when(is_cot)
            def _():
                acc_u[...] += dot_nt(xbuf[u3].reshape(512, cw), wdn[chunk])

                @pl.when(chunk >= 2)
                def _():
                    q_copy(u3).wait()

                @pl.loop(0, NARROW)
                def _(piece):
                    g = gbuf[piece].astype(F32)
                    g = jnp.concatenate([g] * (cw // 128), axis=1)
                    qbuf[u3 % 2, piece] = (g * xbuf[u3, piece].astype(F32)).astype(BF16)

                q_copy(u3).start()

            @pl.when(jnp.logical_not(is_cot))
            def _():
                x_copy(u3).start()
                acc_ab[...] += dot_nt(xbuf[u3].reshape(512, cw), wab[chunk])

    def hidden(r):
        span = slice(r * 128, (r + 1) * 128)
        g = gbuf[2 * r : 2 * r + 2].reshape(128, 128).astype(F32)
        g = jnp.concatenate([g, g], axis=1)
        a = acc_ab[span, 0:PAD]
        b = acc_ab[span, PAD : 2 * PAD]
        u = acc_u[span, :]
        s = jax.nn.sigmoid(a)
        act = a * s
        dh = g * u
        da = dh * b * s * (1.0 + a * (1.0 - s))
        du = dh * act
        h = act * b
        dd[span, 0:PAD] = da.astype(BF16)
        dd[span, PAD : 2 * PAD] = du.astype(BF16)
        acc_ab[span, 0:PAD] = h
        acc_u[span, :] = u * h

    for r in range(4):
        hidden(r)

    ddt_copy = pltpu.make_async_copy(dd_t, ddt_hbm, out_sem.at[1])
    hqt_copy = pltpu.make_async_copy(hq_t, hqt_hbm, out_sem.at[2])

    def turn():
        gp[4:8] = jnp.zeros((4, 128), F32)
        for r in range(4):
            span = slice(r * 128, (r + 1) * 128)
            dd_t[:, span] = dd[span, :].astype(F32).T.astype(BF16)
            hq_t[:, span] = acc_ab[span, 0:PAD].T.astype(BF16)
            gp[r : r + 1, :] = jnp.sum(acc_u[span, :].T, axis=0, keepdims=True)
        ddt_copy.start()
        hqt_copy.start()
        gpr[n] = gp[...]

        @pl.loop(1, NARROW)
        def _(i):
            gp_copy(i).start()

    def gp_copy(i):
        return remote(gp, gpr.at[n], g_s.at[2], g_r.at[2], w, (n + i) % NARROW)

    def gr_copy(i):
        e = (w + i) % WIDE
        return remote(gsum, gret.at[w], g_s.at[3], g_r.at[3], e, n)

    lo, hi = pl.ds(0, 32), pl.ds(32, 32)

    def c_copy(k, s, piece, slot, to_n):
        return remote(
            pbuf.at[k, piece], rb.at[k, slot], c_s.at[k // 7], c_r.at[k, s], w, to_n
        )

    def c_half(k, s, piece, slot, span, to_n):
        return remote(
            pbuf.at[k, piece, span], rb.at[k, slot, span], c_s.at[k // 7], c_r.at[k, s], w, to_n
        )

    def add_into(k, piece, slot, span=slice(None)):
        pbuf[k, piece, span] = (
            pbuf[k, piece, span].astype(F32) + rb[k, slot, span].astype(F32)
        ).astype(BF16)

    def red_a(k):
        return (
            (
                part(c_copy, k, 0, at(y2, 0), 0, dev_p),
                part(c_copy, k, 0, at(y2, 1), 1, dev_m),
                part(c_copy, k, 1, at(yp, 1), 3, dev_p),
                part(c_copy, k, 1, at(ym, 0), 4, dev_m),
            ),
            (
                part(c_copy, k, 1, at(yp, 0), 2, dev_p),
                part(c_copy, k, 1, at(ym, 1), 5, dev_m),
            ),
            (part(c_copy, k, 2, at(y, ox), 6, dev_x),),
        )

    def red_b(k):
        return (
            tuple(part(c_copy, k, 0, at(yy, ox), yy, dev_x) for yy in range(4)),
            (
                part(c_half, k, 1, at(y2, xh), 4, lo, dev_p),
                part(c_half, k, 1, at(y2, xh), 4, hi, dev_m),
                part(c_half, k, 2, at(yp, xh), 5, hi, dev_p),
                part(c_half, k, 2, at(ym, xh), 6, lo, dev_m),
            ),
            (
                part(c_half, k, 2, at(yp, xh), 5, lo, dev_p),
                part(c_half, k, 2, at(ym, xh), 6, hi, dev_m),
            ),
        )

    def ret_copy(g, i):
        to = (w + i) % WIDE
        return remote(
            retsend.at[g, to],
            ret_hbm.at[g, w],
            ret_s.at[g],
            ret_r.at[g],
            to,
            at(y, xh ^ swap(to, w)),
        )

    def own_copy(g):
        return pltpu.make_async_copy(retsend.at[g, w], ret_hbm.at[g, w], out_sem.at[3])

    clag1, clag2, clag3 = REDUCE_LAG

    @pl.loop(0, CHUNKS + clag3)
    def _(t):
        @pl.when(t < CHUNKS)
        def _():
            pbuf[t] = dot(dd[...], wab[t]).astype(BF16).reshape(NARROW, ROWS, cw)

            @pl.when(reduce_is_b(t))
            def _():
                start_all(red_b(t)[0])

            @pl.when(jnp.logical_not(reduce_is_b(t)))
            def _():
                start_all(red_a(t)[0])

        k1 = t - clag1

        @pl.when((k1 >= 0) & (k1 < CHUNKS))
        def _():
            @pl.when(reduce_is_b(k1))
            def _():
                landed(rb.at[k1, pl.ds(0, 4)], c_r.at[k1, 0])
                for yy in (y2, yp, ym):
                    add_into(k1, at(yy, xh), yy)
                start_all(red_b(k1)[1])
                fin[k1] = pbuf[k1, n].astype(F32) + rb[k1, y].astype(F32)

            @pl.when(jnp.logical_not(reduce_is_b(k1)))
            def _():
                landed(rb.at[k1, pl.ds(0, 2)], c_r.at[k1, 0])
                add_into(k1, at(yp, 0), 0)
                add_into(k1, at(ym, 1), 1)
                start_all(red_a(k1)[1])

        k2 = t - clag2

        @pl.when((k2 >= 0) & (k2 < CHUNKS))
        def _():
            @pl.when(reduce_is_b(k2))
            def _():
                landed(rb.at[k2, 4], c_r.at[k2, 1])
                add_into(k2, at(yp, xh), 4, lo)
                add_into(k2, at(ym, xh), 4, hi)
                start_all(red_b(k2)[2])

            @pl.when(jnp.logical_not(reduce_is_b(k2)))
            def _():
                landed(rb.at[k2, pl.ds(2, 4)], c_r.at[k2, 1])
                other = at(y, ox)
                pbuf[k2, other] = (
                    pbuf[k2, other].astype(F32)
                    + rb[k2, 2 + ox].astype(F32)
                    + rb[k2, 4 + ox].astype(F32)
                ).astype(BF16)
                start_all(red_a(k2)[2])
                fin[k2] = (
                    pbuf[k2, n].astype(F32)
                    + rb[k2, 2 + xh].astype(F32)
                    + rb[k2, 4 + xh].astype(F32)
                )

        k3 = t - clag3

        @pl.when(k3 >= 0)
        def _():
            @pl.when(reduce_is_b(k3))
            def _():
                landed(rb.at[k3, pl.ds(5, 2)], c_r.at[k3, 2])
                rbuf[k3] = (
                    fin[k3] + rb[k3, 5].astype(F32) + rb[k3, 6].astype(F32)
                ).astype(BF16)

            @pl.when(jnp.logical_not(reduce_is_b(k3)))
            def _():
                landed(rb.at[k3, 6], c_r.at[k3, 2])
                rbuf[k3] = (fin[k3] + rb[k3, 6].astype(F32)).astype(BF16)

            @pl.when(k3 % 2 == 1)
            def _():
                g = k3 // 2
                rows = jnp.concatenate(
                    [
                        rbuf[2 * g + q // 2, :, (q % 2) * qw : (q % 2 + 1) * qw]
                        for q in range(4)
                    ],
                    axis=0,
                )
                retsend[g] = dot(unsort_rows, rows).astype(BF16).reshape(WIDE, 16, qw)

                @pl.loop(1, WIDE)
                def _(i):
                    ret_copy(g, i).start()

                own_copy(g).start()

        @pl.when(t == 1)
        def _():
            turn()

        @pl.when(t == 6)
        def _():
            landed(gpr.at[pl.ds(0, NARROW - 1)], g_r.at[2])
            gsum[...] = jnp.sum(gpr[...], axis=0)
            gret[w] = gsum[...]

            @pl.loop(1, WIDE)
            def _(i):
                gr_copy(i).start()

    landed(gret.at[pl.ds(0, WIDE - 1)], g_r.at[3])

    row64 = iota((ROWS, WIDE), 0)
    spread = jnp.where((row64 >> 2) == iota((ROWS, WIDE), 1), 1.0, 0.0)
    line = gret[:, y, :]
    table = lax.dot_general(
        spread,
        line,
        (((1,), (0,)), ((), ())),
        precision=lax.Precision.HIGHEST,
        preferred_element_type=F32,
    )
    slot_row = iota((ROWS, 128), 0)
    turned = (((slot_row >> 3) & 1) ^ xl) & core
    lane = (xh ^ turned) * ROWS + w * CAP + (slot_row & 3)
    column = jnp.sum(
        jnp.where(iota((ROWS, 128), 1) == lane, table, 0.0), axis=1, keepdims=True
    )
    for k in range(8):
        match = target[k : k + 1, :] == slot_row
        gg_ref[k : k + 1, :] = jnp.sum(jnp.where(match, column, 0.0), axis=0, keepdims=True)

    sent(gsend.at[pl.ds(0, WIDE - 1)], g_s.at[0])
    sent(gbuf.at[pl.ds(0, NARROW - 1)], g_s.at[1])
    sent(gpr.at[pl.ds(0, NARROW - 1)], g_s.at[2])
    sent(gret.at[pl.ds(0, WIDE - 1)], g_s.at[3])
    for i in range(4):
        sent(xbuf.at[pl.ds(i * 7, 7), pl.ds(0, 7)], ag_s.at[i])
    for i in range(2):
        sent(pbuf.at[pl.ds(i * 7, 7), pl.ds(0, 7)], c_s.at[i])
    here(xbuf.at[pl.ds(0, CHUNKS)], x_sem.at[0])
    for k in range(2):
        q_copy(UNITS - 2 + k).wait()
    placet_copy.wait()
    ddt_copy.wait()
    hqt_copy.wait()

    @pl.loop(0, STAGES)
    def _(g):
        sent(sendbuf.at[g, pl.ds(0, WIDE - 1)], a2a_s.at[g])
        sent(retsend.at[g, pl.ds(0, WIDE - 1)], ret_s.at[g])
        landed(retsend.at[g, pl.ds(0, WIDE - 1)], ret_r.at[g])

    here(retsend.at[:, 0], out_sem.at[3])


def finish(
    ddt_ref, hqt_ref, placet_ref, gg_ref, ret_ref, x_ref, q_ref, gt_ref, gg_out, og_ref, ou_ref, od_ref
):
    hid = og_ref.shape[1]
    cw = x_ref.shape[2]
    qw = cw // 2
    for half in range(2):
        span = slice(half * cw, (half + 1) * cw)
        both = dot(ddt_ref[...], x_ref[half]).astype(BF16)
        og_ref[0, :, span] = both[0:hid]
        ou_ref[0, :, span] = both[PAD : PAD + hid]
        od_ref[0, :, span] = dot(hqt_ref[...], q_ref[half]).astype(BF16)[0:hid]
    home = dot(placet_ref[...], ret_ref[0]).astype(BF16)
    for q in range(4):
        gt_ref[:, q * qw : (q + 1) * qw] = home[q * 128 : (q + 1) * 128]
    gg_out[...] = gg_ref[...]


def per_device(tokens, grad_out, gates, expert_ids, slots, w_gate, w_up, w_down):
    width = tokens.shape[1]
    cw = width // CHUNKS
    any_spec = pl.BlockSpec(memory_space=pl.ANY)
    vmem_spec = pl.BlockSpec(memory_space=pltpu.VMEM)
    vm = pltpu.VMEM
    dma = pltpu.SemaphoreType.DMA
    sds = jax.ShapeDtypeStruct
    xq, ddt, hqt, placet, ret, gg = pl.pallas_call(
        kernel,
        out_shape=(
            sds((UNITS, NARROW, ROWS, cw), BF16),
            sds((2 * PAD, 512), BF16),
            sds((PAD, 512), BF16),
            sds((512, 256), BF16),
            sds((STAGES, WIDE, 16, cw // 2), BF16),
            sds((8, 128), F32),
        ),
        in_specs=[vmem_spec] * 3 + [any_spec] * 5,
        out_specs=(any_spec,) * 5 + (vmem_spec,),
        scratch_shapes=[
            vm((256, 512), BF16),
            vm((512, 256), BF16),
            vm((STAGES, 2, 128, 2 * cw), BF16),
            vm((STAGES, WIDE, 2, 16, cw // 2), BF16),
            vm((STAGES, WIDE, 2, 16, cw // 2), BF16),
            vm((UNITS, NARROW, ROWS, cw), BF16),
            vm((CHUNKS, 2 * PAD, cw), BF16),
            vm((CHUNKS, PAD, cw), BF16),
            vm((512, 2 * PAD), F32),
            vm((512, PAD), F32),
            vm((WIDE, 16, 128), BF16),
            vm((WIDE, 16, 128), BF16),
            vm((NARROW, ROWS, 128), BF16),
            vm((512, 2 * PAD), BF16),
            vm((2 * PAD, 512), BF16),
            vm((PAD, 512), BF16),
            vm((CHUNKS, NARROW, ROWS, cw), BF16),
            vm((CHUNKS, 7, ROWS, cw), BF16),
            vm((CHUNKS, ROWS, cw), F32),
            vm((CHUNKS, ROWS, cw), BF16),
            vm((STAGES, WIDE, 16, cw // 2), BF16),
            vm((2, NARROW, ROWS, cw), BF16),
            vm((8, 128), F32),
            vm((NARROW, 8, 128), F32),
            vm((8, 128), F32),
            vm((WIDE, 8, 128), F32),
            dma((STAGES,)),
            dma((2,)),
            dma((STAGES,)),
            dma((STAGES,)),
            dma((4,)),
            dma((4,)),
            dma((4,)),
            dma((UNITS, 3)),
            dma((2,)),
            dma((CHUNKS, 3)),
            dma((STAGES,)),
            dma((STAGES,)),
            dma((1,)),
            dma((2,)),
            dma((4,)),
        ],
        compiler_params=pltpu.CompilerParams(
            collective_id=0, has_side_effects=True, vmem_limit_bytes=63 * 2**20
        ),
        name="routed_backward",
    )(
        expert_ids.T,
        slots.T,
        gates.T,
        tokens,
        grad_out,
        w_gate,
        w_up,
        w_down,
    )
    xq = xq.reshape(UNITS, 512, cw)
    ret = ret.reshape(STAGES, 256, cw // 2)
    hid = w_gate.shape[1]

    def whole(shape):
        return pl.BlockSpec(shape, lambda g: (0,) * len(shape))

    weight_block = pl.BlockSpec((1, hid, 2 * cw), lambda g: (0, 0, g))
    gt, gg, og, ou, od = pl.pallas_call(
        finish,
        grid=(STAGES,),
        in_specs=[
            whole((2 * PAD, 512)),
            whole((PAD, 512)),
            whole((512, 256)),
            whole((8, 128)),
            pl.BlockSpec((1, 256, cw // 2), lambda g: (g, 0, 0)),
            pl.BlockSpec((2, 512, cw), lambda g: (2 * g, 0, 0)),
            pl.BlockSpec((2, 512, cw), lambda g: (2 * g + 1, 0, 0)),
        ],
        out_specs=[
            pl.BlockSpec((128, 2 * cw), lambda g: (0, g)),
            whole((8, 128)),
            weight_block,
            weight_block,
            weight_block,
        ],
        out_shape=[
            sds(tokens.shape, BF16),
            sds((8, 128), F32),
            sds(w_gate.shape, BF16),
            sds(w_up.shape, BF16),
            sds(w_down.shape, BF16),
        ],
        compiler_params=pltpu.CompilerParams(vmem_limit_bytes=62 * 2**20),
        name="weight_grads",
    )(ddt, hqt, placet, gg, ret, xq, xq)
    return (gt, gg.T, og, ou, od)


def solution(mesh):
    rows = P(("wide", "narrow"), None)
    weights = P("wide", "narrow", None)
    return jax.shard_map(
        per_device,
        mesh=mesh,
        in_specs=(rows,) * 5 + (weights,) * 3,
        out_specs=(rows, rows, weights, weights, weights),
        check_vma=False,
    )
```

time: 220 us -> 196 us (0.89)
  local copies, waits for them, and re-layouts: 11.4 us -> 0 us
  Pallas kernels: 206 us -> 195 us
    unnamed x13 -> x0, local copies, waits for them, and re-layouts: 11.4 us -> none
    pallas_call x1 -> x2, Pallas kernels: 206 us -> 195 us  [the longest x1 180 us: per_device(): pl.pallas_call(kernel, out_shape=(sds((UNITS, NARROW, ROWS, cw), BF16), s...]
where the time goes in v2:
time: 196 us; the launch traced here: 195 us
  Pallas kernels  195 us (99%)
    pallas_call x1, Pallas kernels, per_device(): pl.pallas_call(kernel, out_shape=(sds((UNITS, NARROW, ROWS, cw), BF16), s...  180 us
    pallas_call x1, Pallas kernels, per_device(): pl.pallas_call(finish, grid=(STAGES,), in_specs=[whole((2 * PAD, 512)), w...  14.2 us

profile of v2, /device:TPU:1, one launch (start us, length us, event | category | flops | bytes accessed | tf_op | source)
XLA Modules:
  0.0 195.2 jit_solution(10696065209397324859)
XLA Ops:
  0.6 180.4 %routed_backward.1 = (bf16[28,8,64,512]{3,2,1,0:T(8,128)(2,1)}, bf16[512,512]{1,0:T(8,128)(2,1)}, bf16[256,512]{1,0:T(8,128)(2,1)}, bf16[512,256]{1,0:T(8,128)(2...) custom-call(s32[8,128]{1,0:T(8,128)} %bitcast.9, s32[8,128]{1,0:T(8,128)} %bitcast.10, bf16[8,128]{1,0:T(8,128)(2,1)} %bitcast.11, ...), custom_call_target="tpu_custom_call" | custom-call | tf_op jit(solution)/shard_map/routed_backward/pallas_call | solution.py:718
  181.0 14.2 %weight_grads.1 = (bf16[128,7168]{1,0:T(8,128)(2,1)}, f32[8,128]{1,0:T(8,128)}, bf16[1,224,7168]{2,1,0:T(8,128)(2,1)}, bf16[1,224,7168]{2,1,0:T(8,128)(2,1)}, bf16[1,224,7168]{2,1,0:T(8,128)(2,1)}) custom-call(bf16[512,512]{1,0:T(8,128)(2,1)} %get-tuple-element.16.ddt_ref, bf16[256,512]{1,0:T(8,128)(2,1)} %get-tuple-element.17.hqt_ref, ...), custom_call_target="tpu_custom_call" | custom-call | tf_op jit(solution)/shard_map/weight_grads/pallas_call | solution.py:795

commit v3 on v2

--- a/solution.py
+++ b/solution.py
@@ -15,7 +15,8 @@
 CHUNKS = 2 * STAGES
 UNITS = 2 * CHUNKS
 GATHER_LAG = (2, 4, 6)
-REDUCE_LAG = (2, 4, 6)
+REDUCE_LAG = (4, 8, 12)
+GRADS_LAG = 3
 PAD = 256
 MESH = pl.DeviceIdType.MESH
 F32 = jnp.float32
@@ -35,11 +36,11 @@
 
 
 def gather_is_b(unit):
-    return (unit * 11 + 17) % 28 < 11
+    return (unit * 11) % 28 < 11
 
 
 def reduce_is_b(chunk):
-    return (chunk * 5) % 14 < 5
+    return (chunk * 5 + 9) % 14 < 5
 
 
 def kernel(
@@ -51,9 +52,9 @@
     wg_hbm,
     wu_hbm,
     wd_hbm,
-    xq_hbm,
-    ddt_hbm,
-    hqt_hbm,
+    og_hbm,
+    ou_hbm,
+    od_hbm,
     placet_hbm,
     ret_hbm,
     gg_ref,
@@ -79,6 +80,8 @@
     rbuf,
     retsend,
     qbuf,
+    stage_ab,
+    stage_d,
     gp,
     gpr,
     gsum,
@@ -95,8 +98,7 @@
     c_r,
     ret_s,
     ret_r,
-    x_sem,
-    q_sem,
+    grad_sem,
     out_sem,
 ):
     w = lax.axis_index("wide")
@@ -200,8 +202,6 @@
         dot(weight.astype(BF16), jnp.ones((128, 128), BF16)).astype(BF16).reshape(WIDE, 16, 128)
     )
 
-    pl.semaphore_wait(barrier, 2 * WIDE - 1 + NARROW - 2)
-
     def a2a_copy(g, i):
         e = (w + i) % WIDE
         return remote(
@@ -225,6 +225,7 @@
             )
             sendbuf[g, :, arr] = dot(place[...], slab).astype(BF16).reshape(WIDE, 16, qw)
 
+    def post(g):
         @pl.loop(1, WIDE)
         def _(i):
             a2a_copy(g, i).start()
@@ -232,6 +233,8 @@
         a2abuf[g, w] = sendbuf[g, w]
 
     pack(0)
+    pl.semaphore_wait(barrier, 2 * WIDE - 1 + NARROW - 2)
+    post(0)
 
     @pl.loop(1, WIDE)
     def _(i):
@@ -315,12 +318,7 @@
     def gg_copy(i):
         return remote(gbuf.at[n], gbuf.at[n], g_s.at[1], g_r.at[1], w, (n + i) % NARROW)
 
-    def x_copy(u):
-        return pltpu.make_async_copy(xbuf.at[u], xq_hbm.at[u], x_sem.at[0])
-
-    def q_copy(u):
-        return pltpu.make_async_copy(qbuf.at[u % 2], xq_hbm.at[u], q_sem.at[u % 2])
-
+    pack(1)
     lag1, lag2, lag3 = GATHER_LAG
 
     @pl.loop(0, UNITS + lag3)
@@ -341,11 +339,12 @@
 
         @pl.when(t == 0)
         def _():
-            pack(1)
+            post(1)
 
         @pl.when((t % 4 == 1) & (t // 4 + 2 < STAGES))
         def _():
             pack(t // 4 + 2)
+            post(t // 4 + 2)
 
         @pl.when(t == 3)
         def _():
@@ -409,21 +408,8 @@
             def _():
                 acc_u[...] += dot_nt(xbuf[u3].reshape(512, cw), wdn[chunk])
 
-                @pl.when(chunk >= 2)
-                def _():
-                    q_copy(u3).wait()
-
-                @pl.loop(0, NARROW)
-                def _(piece):
-                    g = gbuf[piece].astype(F32)
-                    g = jnp.concatenate([g] * (cw // 128), axis=1)
-                    qbuf[u3 % 2, piece] = (g * xbuf[u3, piece].astype(F32)).astype(BF16)
-
-                q_copy(u3).start()
-
             @pl.when(jnp.logical_not(is_cot))
             def _():
-                x_copy(u3).start()
                 acc_ab[...] += dot_nt(xbuf[u3].reshape(512, cw), wab[chunk])
 
     def hidden(r):
@@ -447,9 +433,6 @@
     for r in range(4):
         hidden(r)
 
-    ddt_copy = pltpu.make_async_copy(dd_t, ddt_hbm, out_sem.at[1])
-    hqt_copy = pltpu.make_async_copy(hq_t, hqt_hbm, out_sem.at[2])
-
     def turn():
         gp[4:8] = jnp.zeros((4, 128), F32)
         for r in range(4):
@@ -457,8 +440,6 @@
             dd_t[:, span] = dd[span, :].astype(F32).T.astype(BF16)
             hq_t[:, span] = acc_ab[span, 0:PAD].T.astype(BF16)
             gp[r : r + 1, :] = jnp.sum(acc_u[span, :].T, axis=0, keepdims=True)
-        ddt_copy.start()
-        hqt_copy.start()
         gpr[n] = gp[...]
 
         @pl.loop(1, NARROW)
@@ -531,7 +512,21 @@
         )
 
     def own_copy(g):
-        return pltpu.make_async_copy(retsend.at[g, w], ret_hbm.at[g, w], out_sem.at[3])
+        return pltpu.make_async_copy(retsend.at[g, w], ret_hbm.at[g, w], out_sem.at[1])
+
+    def grad_copies(k):
+        slot = k % 2
+        return (
+            pltpu.make_async_copy(
+                stage_ab.at[slot, pl.ds(0, hid)], og_hbm.at[0, :, cols(k)], grad_sem.at[slot]
+            ),
+            pltpu.make_async_copy(
+                stage_ab.at[slot, pl.ds(PAD, hid)], ou_hbm.at[0, :, cols(k)], grad_sem.at[slot]
+            ),
+            pltpu.make_async_copy(
+                stage_d.at[slot, pl.ds(0, hid)], od_hbm.at[0, :, cols(k)], grad_sem.at[slot]
+            ),
+        )
 
     clag1, clag2, clag3 = REDUCE_LAG
 
@@ -632,6 +627,30 @@
         @pl.when(t == 1)
         def _():
             turn()
+
+        kw = t - GRADS_LAG
+
+        @pl.when((kw >= 0) & (kw < CHUNKS))
+        def _():
+            slot = kw % 2
+
+            @pl.when(kw >= 2)
+            def _():
+                for cp in grad_copies(kw):
+                    cp.wait()
+
+            unit = (kw // 2) * 4 + kw % 2
+            stage_ab[slot] = dot(dd_t[...], xbuf[unit].reshape(512, cw)).astype(BF16)
+
+            @pl.loop(0, NARROW)
+            def _(piece):
+                g = gbuf[piece].astype(F32)
+                g = jnp.concatenate([g] * (cw // 128), axis=1)
+                qbuf[piece] = (g * xbuf[unit + 2, piece].astype(F32)).astype(BF16)
+
+            stage_d[slot] = dot(hq_t[...], qbuf[...].reshape(512, cw)).astype(BF16)
+            for cp in grad_copies(kw):
+                cp.start()
 
         @pl.when(t == 6)
         def _():
@@ -673,12 +692,10 @@
         sent(xbuf.at[pl.ds(i * 7, 7), pl.ds(0, 7)], ag_s.at[i])
     for i in range(2):
         sent(pbuf.at[pl.ds(i * 7, 7), pl.ds(0, 7)], c_s.at[i])
-    here(xbuf.at[pl.ds(0, CHUNKS)], x_sem.at[0])
-    for k in range(2):
-        q_copy(UNITS - 2 + k).wait()
+    for k in range(CHUNKS - 2, CHUNKS):
+        for cp in grad_copies(k):
+            cp.wait()
     placet_copy.wait()
-    ddt_copy.wait()
-    hqt_copy.wait()
 
     @pl.loop(0, STAGES)
     def _(g):
@@ -686,25 +703,69 @@
         sent(retsend.at[g, pl.ds(0, WIDE - 1)], ret_s.at[g])
         landed(retsend.at[g, pl.ds(0, WIDE - 1)], ret_r.at[g])
 
-    here(retsend.at[:, 0], out_sem.at[3])
+    here(retsend.at[:, 0], out_sem.at[1])
 
 
 def finish(
-    ddt_ref, hqt_ref, placet_ref, gg_ref, ret_ref, x_ref, q_ref, gt_ref, gg_out, og_ref, ou_ref, od_ref
+    placet_hbm,
+    gg_ref,
+    ret_hbm,
+    og_in,
+    ou_in,
+    od_in,
+    gt_hbm,
+    gg_out,
+    og_hbm,
+    ou_hbm,
+    od_hbm,
+    placet,
+    ret,
+    gt,
+    held,
+    small_sem,
+    in_sem,
+    out_sem,
+    gt_sem,
 ):
-    hid = og_ref.shape[1]
-    cw = x_ref.shape[2]
-    qw = cw // 2
-    for half in range(2):
-        span = slice(half * cw, (half + 1) * cw)
-        both = dot(ddt_ref[...], x_ref[half]).astype(BF16)
-        og_ref[0, :, span] = both[0:hid]
-        ou_ref[0, :, span] = both[PAD : PAD + hid]
-        od_ref[0, :, span] = dot(hqt_ref[...], q_ref[half]).astype(BF16)[0:hid]
-    home = dot(placet_ref[...], ret_ref[0]).astype(BF16)
-    for q in range(4):
-        gt_ref[:, q * qw : (q + 1) * qw] = home[q * 128 : (q + 1) * 128]
+    qw = ret.shape[2]
+    step = 32
+    parts = held.shape[1] // step
+    rows_in = (
+        pltpu.make_async_copy(placet_hbm, placet, small_sem.at[0]),
+        pltpu.make_async_copy(ret_hbm, ret, small_sem.at[1]),
+    )
+    loads, stores = [], []
+    for i, (src, dst) in enumerate(((og_in, og_hbm), (ou_in, ou_hbm), (od_in, od_hbm))):
+        for j in range(parts):
+            span = pl.ds(j * step, step)
+            here = held.at[i, span]
+            loads.append(pltpu.make_async_copy(src.at[0, span], here, in_sem.at[i, j]))
+            stores.append(pltpu.make_async_copy(here, dst.at[0, span], out_sem.at[i, j]))
+    for cp in loads[:parts]:
+        cp.start()
+    for cp in rows_in:
+        cp.start()
+    for cp in loads[parts:]:
+        cp.start()
     gg_out[...] = gg_ref[...]
+    for load, store in zip(loads[:parts], stores[:parts]):
+        load.wait()
+        store.start()
+    for cp in rows_in:
+        cp.wait()
+    homes = []
+    for g in range(STAGES):
+        home = dot(placet[...], ret[g]).astype(BF16)
+        for q in range(4):
+            gt[:, (g * 4 + q) * qw : (g * 4 + q + 1) * qw] = home[q * 128 : (q + 1) * 128]
+        span = pl.ds(g * 4 * qw, 4 * qw)
+        homes.append(pltpu.make_async_copy(gt.at[:, span], gt_hbm.at[:, span], gt_sem.at[g]))
+        homes[-1].start()
+        for k in range(parts + 2 * g, parts + 2 * g + 2):
+            loads[k].wait()
+            stores[k].start()
+    for cp in stores + homes:
+        cp.wait()
 
 
 def per_device(tokens, grad_out, gates, expert_ids, slots, w_gate, w_up, w_down):
@@ -715,12 +776,12 @@
     vm = pltpu.VMEM
     dma = pltpu.SemaphoreType.DMA
     sds = jax.ShapeDtypeStruct
-    xq, ddt, hqt, placet, ret, gg = pl.pallas_call(
+    og, ou, od, placet, ret, gg = pl.pallas_call(
         kernel,
         out_shape=(
-            sds((UNITS, NARROW, ROWS, cw), BF16),
-            sds((2 * PAD, 512), BF16),
-            sds((PAD, 512), BF16),
+            sds(w_gate.shape, BF16),
+            sds(w_up.shape, BF16),
+            sds(w_down.shape, BF16),
             sds((512, 256), BF16),
             sds((STAGES, WIDE, 16, cw // 2), BF16),
             sds((8, 128), F32),
@@ -749,7 +810,9 @@
             vm((CHUNKS, ROWS, cw), F32),
             vm((CHUNKS, ROWS, cw), BF16),
             vm((STAGES, WIDE, 16, cw // 2), BF16),
-            vm((2, NARROW, ROWS, cw), BF16),
+            vm((NARROW, ROWS, cw), BF16),
+            vm((2, 2 * PAD, cw), BF16),
+            vm((2, PAD, cw), BF16),
             vm((8, 128), F32),
             vm((NARROW, 8, 128), F32),
             vm((8, 128), F32),
@@ -766,9 +829,8 @@
             dma((CHUNKS, 3)),
             dma((STAGES,)),
             dma((STAGES,)),
-            dma((1,)),
             dma((2,)),
-            dma((4,)),
+            dma((2,)),
         ],
         compiler_params=pltpu.CompilerParams(
             collective_id=0, has_side_effects=True, vmem_limit_bytes=63 * 2**20
@@ -784,43 +846,31 @@
         w_up,
         w_down,
     )
-    xq = xq.reshape(UNITS, 512, cw)
     ret = ret.reshape(STAGES, 256, cw // 2)
-    hid = w_gate.shape[1]
-
-    def whole(shape):
-        return pl.BlockSpec(shape, lambda g: (0,) * len(shape))
-
-    weight_block = pl.BlockSpec((1, hid, 2 * cw), lambda g: (0, 0, g))
     gt, gg, og, ou, od = pl.pallas_call(
         finish,
-        grid=(STAGES,),
-        in_specs=[
-            whole((2 * PAD, 512)),
-            whole((PAD, 512)),
-            whole((512, 256)),
-            whole((8, 128)),
-            pl.BlockSpec((1, 256, cw // 2), lambda g: (g, 0, 0)),
-            pl.BlockSpec((2, 512, cw), lambda g: (2 * g, 0, 0)),
-            pl.BlockSpec((2, 512, cw), lambda g: (2 * g + 1, 0, 0)),
-        ],
-        out_specs=[
-            pl.BlockSpec((128, 2 * cw), lambda g: (0, g)),
-            whole((8, 128)),
-            weight_block,
-            weight_block,
-            weight_block,
-        ],
-        out_shape=[
+        in_specs=[any_spec, vmem_spec] + [any_spec] * 4,
+        out_specs=(any_spec, vmem_spec) + (any_spec,) * 3,
+        out_shape=(
             sds(tokens.shape, BF16),
             sds((8, 128), F32),
             sds(w_gate.shape, BF16),
             sds(w_up.shape, BF16),
             sds(w_down.shape, BF16),
+        ),
+        scratch_shapes=[
+            vm((512, 256), BF16),
+            vm((STAGES, 256, cw // 2), BF16),
+            vm(tokens.shape, BF16),
+            vm((3,) + w_gate.shape[1:], BF16),
+            dma((2,)),
+            dma((3, 7)),
+            dma((3, 7)),
+            dma((STAGES,)),
         ],
         compiler_params=pltpu.CompilerParams(vmem_limit_bytes=62 * 2**20),
-        name="weight_grads",
-    )(ddt, hqt, placet, gg, ret, xq, xq)
+        name="finish",
+    )(placet, gg, ret, og, ou, od)
     return (gt, gg.T, og, ou, od)
 
 

time: 196 us -> 187 us (0.954)
  Pallas kernels: 195 us -> 186 us
    pallas_call x2, Pallas kernels: 195 us -> 186 us  [the longest x1 175 us: per_device(): pl.pallas_call(kernel, out_shape=(sds(w_gate.shape, BF16), sds(w_up.shape...]
where the time goes in v3:
time: 187 us; the launch traced here: 186 us
  Pallas kernels  186 us (99%)
    pallas_call x1, Pallas kernels, per_device(): pl.pallas_call(kernel, out_shape=(sds(w_gate.shape, BF16), sds(w_up.shape...  175 us
    pallas_call x1, Pallas kernels, per_device(): pl.pallas_call(finish, in_specs=[any_spec, vmem_spec] + [any_spec] * 4, o...  10.3 us

profile of v3, /device:TPU:1, one launch (start us, length us, event | category | flops | bytes accessed | tf_op | source)
XLA Modules:
  0.0 186.4 jit_solution(5450890145661471576)
XLA Ops:
  0.6 175.4 %routed_backward.1 = (bf16[1,224,7168]{2,1,0:T(8,128)(2,1)}, bf16[1,224,7168]{2,1,0:T(8,128)(2,1)}, bf16[1,224,7168]{2,1,0:T(8,128)(2,1)}, bf16[512,256]{1,0:T(8...) custom-call(s32[8,128]{1,0:T(8,128)} %bitcast.6, s32[8,128]{1,0:T(8,128)} %bitcast.7, ...), custom_call_target="tpu_custom_call" | custom-call | tf_op jit(solution)/shard_map/routed_backward/pallas_call | solution.py:779
  176.1 10.3 %finish.1 = (bf16[128,7168]{1,0:T(8,128)(2,1)}, f32[8,128]{1,0:T(8,128)}, bf16[1,224,7168]{2,1,0:T(8,128)(2,1)}, bf16[1,224,7168]{2,1,0:T(8,128)(2,1)}, bf16[1,224,7168]{2,1,0:T(8,128)(2,1)}) custom-call(bf16[512,256]{1,0:T(8,128)(2,1)} %get-tuple-element.16.placet_hbm, f32[8,128]{1,0:T(8,128)} %get-tuple-element.17.gg_ref, bf16[7,256,256]{2,1,0:T(8,128)(2,1)} %bitcast.5, ...), custom_call_target="tpu_custom_call" | custom-call | tf_op jit(solution)/shard_map/finish/pallas_call | solution.py:850

commit v4 on v3

--- a/solution.py
+++ b/solution.py
@@ -16,7 +16,7 @@
 UNITS = 2 * CHUNKS
 GATHER_LAG = (2, 4, 6)
 REDUCE_LAG = (4, 8, 12)
-GRADS_LAG = 3
+GRADS_LAG = 4
 PAD = 256
 MESH = pl.DeviceIdType.MESH
 F32 = jnp.float32
@@ -57,7 +57,7 @@
     od_hbm,
     placet_hbm,
     ret_hbm,
-    gg_ref,
+    gg_hbm,
     place,
     place_t,
     tokbuf,
@@ -86,6 +86,7 @@
     gpr,
     gsum,
     gret,
+    gg_ref,
     tok_sem,
     w_sem,
     a2a_s,
@@ -528,6 +529,32 @@
             ),
         )
 
+    gg_copy_out = pltpu.make_async_copy(gg_ref, gg_hbm, out_sem.at[2])
+
+    def router():
+        landed(gret.at[pl.ds(0, WIDE - 1)], g_r.at[3])
+
+        row64 = iota((ROWS, WIDE), 0)
+        spread = jnp.where((row64 >> 2) == iota((ROWS, WIDE), 1), 1.0, 0.0)
+        line = gret[:, y, :]
+        table = lax.dot_general(
+            spread,
+            line,
+            (((1,), (0,)), ((), ())),
+            precision=lax.Precision.HIGHEST,
+            preferred_element_type=F32,
+        )
+        slot_row = iota((ROWS, 128), 0)
+        turned = (((slot_row >> 3) & 1) ^ xl) & core
+        lane = (xh ^ turned) * ROWS + w * CAP + (slot_row & 3)
+        column = jnp.sum(
+            jnp.where(iota((ROWS, 128), 1) == lane, table, 0.0), axis=1, keepdims=True
+        )
+        for k in range(8):
+            match = target[k : k + 1, :] == slot_row
+            gg_ref[k : k + 1, :] = jnp.sum(jnp.where(match, column, 0.0), axis=0, keepdims=True)
+        gg_copy_out.start()
+
     clag1, clag2, clag3 = REDUCE_LAG
 
     @pl.loop(0, CHUNKS + clag3)
@@ -624,9 +651,13 @@
 
                 own_copy(g).start()
 
-        @pl.when(t == 1)
+        @pl.when(t == 3)
         def _():
             turn()
+
+        @pl.when(t == CHUNKS + 4)
+        def _():
+            router()
 
         kw = t - GRADS_LAG
 
@@ -652,7 +683,7 @@
             for cp in grad_copies(kw):
                 cp.start()
 
-        @pl.when(t == 6)
+        @pl.when(t == 9)
         def _():
             landed(gpr.at[pl.ds(0, NARROW - 1)], g_r.at[2])
             gsum[...] = jnp.sum(gpr[...], axis=0)
@@ -661,28 +692,6 @@
             @pl.loop(1, WIDE)
             def _(i):
                 gr_copy(i).start()
-
-    landed(gret.at[pl.ds(0, WIDE - 1)], g_r.at[3])
-
-    row64 = iota((ROWS, WIDE), 0)
-    spread = jnp.where((row64 >> 2) == iota((ROWS, WIDE), 1), 1.0, 0.0)
-    line = gret[:, y, :]
-    table = lax.dot_general(
-        spread,
-        line,
-        (((1,), (0,)), ((), ())),
-        precision=lax.Precision.HIGHEST,
-        preferred_element_type=F32,
-    )
-    slot_row = iota((ROWS, 128), 0)
-    turned = (((slot_row >> 3) & 1) ^ xl) & core
-    lane = (xh ^ turned) * ROWS + w * CAP + (slot_row & 3)
-    column = jnp.sum(
-        jnp.where(iota((ROWS, 128), 1) == lane, table, 0.0), axis=1, keepdims=True
-    )
-    for k in range(8):
-        match = target[k : k + 1, :] == slot_row
-        gg_ref[k : k + 1, :] = jnp.sum(jnp.where(match, column, 0.0), axis=0, keepdims=True)
 
     sent(gsend.at[pl.ds(0, WIDE - 1)], g_s.at[0])
     sent(gbuf.at[pl.ds(0, NARROW - 1)], g_s.at[1])
@@ -696,6 +705,7 @@
         for cp in grad_copies(k):
             cp.wait()
     placet_copy.wait()
+    gg_copy_out.wait()
 
     @pl.loop(0, STAGES)
     def _(g):
@@ -708,7 +718,7 @@
 
 def finish(
     placet_hbm,
-    gg_ref,
+    gg_in,
     ret_hbm,
     og_in,
     ou_in,
@@ -718,6 +728,7 @@
     og_hbm,
     ou_hbm,
     od_hbm,
+    gg,
     placet,
     ret,
     gt,
@@ -733,6 +744,7 @@
     rows_in = (
         pltpu.make_async_copy(placet_hbm, placet, small_sem.at[0]),
         pltpu.make_async_copy(ret_hbm, ret, small_sem.at[1]),
+        pltpu.make_async_copy(gg_in, gg, small_sem.at[2]),
     )
     loads, stores = [], []
     for i, (src, dst) in enumerate(((og_in, og_hbm), (ou_in, ou_hbm), (od_in, od_hbm))):
@@ -747,13 +759,13 @@
         cp.start()
     for cp in loads[parts:]:
         cp.start()
-    gg_out[...] = gg_ref[...]
     for load, store in zip(loads[:parts], stores[:parts]):
         load.wait()
         store.start()
     for cp in rows_in:
         cp.wait()
-    homes = []
+    homes = [pltpu.make_async_copy(gg, gg_out, gt_sem.at[STAGES])]
+    homes[0].start()
     for g in range(STAGES):
         home = dot(placet[...], ret[g]).astype(BF16)
         for q in range(4):
@@ -787,7 +799,7 @@
             sds((8, 128), F32),
         ),
         in_specs=[vmem_spec] * 3 + [any_spec] * 5,
-        out_specs=(any_spec,) * 5 + (vmem_spec,),
+        out_specs=(any_spec,) * 6,
         scratch_shapes=[
             vm((256, 512), BF16),
             vm((512, 256), BF16),
@@ -817,6 +829,7 @@
             vm((NARROW, 8, 128), F32),
             vm((8, 128), F32),
             vm((WIDE, 8, 128), F32),
+            vm((8, 128), F32),
             dma((STAGES,)),
             dma((2,)),
             dma((STAGES,)),
@@ -830,7 +843,7 @@
             dma((STAGES,)),
             dma((STAGES,)),
             dma((2,)),
-            dma((2,)),
+            dma((3,)),
         ],
         compiler_params=pltpu.CompilerParams(
             collective_id=0, has_side_effects=True, vmem_limit_bytes=63 * 2**20
@@ -849,8 +862,8 @@
     ret = ret.reshape(STAGES, 256, cw // 2)
     gt, gg, og, ou, od = pl.pallas_call(
         finish,
-        in_specs=[any_spec, vmem_spec] + [any_spec] * 4,
-        out_specs=(any_spec, vmem_spec) + (any_spec,) * 3,
+        in_specs=[any_spec] * 6,
+        out_specs=(any_spec,) * 5,
         out_shape=(
             sds(tokens.shape, BF16),
             sds((8, 128), F32),
@@ -859,14 +872,15 @@
             sds(w_down.shape, BF16),
         ),
         scratch_shapes=[
+            vm((8, 128), F32),
             vm((512, 256), BF16),
             vm((STAGES, 256, cw // 2), BF16),
             vm(tokens.shape, BF16),
             vm((3,) + w_gate.shape[1:], BF16),
-            dma((2,)),
+            dma((3,)),
             dma((3, 7)),
             dma((3, 7)),
-            dma((STAGES,)),
+            dma((STAGES + 1,)),
         ],
         compiler_params=pltpu.CompilerParams(vmem_limit_bytes=62 * 2**20),
         name="finish",

time: 187 us -> 185 us (0.989)
  Pallas kernels: 186 us -> 184 us
where the time goes in v4:
time: 185 us; the launch traced here: 184 us
  Pallas kernels  184 us (99%)
    pallas_call x1, Pallas kernels, per_device(): pl.pallas_call(kernel, out_shape=(sds(w_gate.shape, BF16), sds(w_up.shape...  175 us
    pallas_call x1, Pallas kernels, per_device(): pl.pallas_call(finish, in_specs=[any_spec] * 6, out_specs=(any_spec,) * 5...  8.94 us

profile of v4, /device:TPU:1, one launch (start us, length us, event | category | flops | bytes accessed | tf_op | source)
XLA Modules:
  0.0 184.4 jit_solution(1172165588742001014)
XLA Ops:
  0.6 174.9 %routed_backward.1 = (bf16[1,224,7168]{2,1,0:T(8,128)(2,1)}, bf16[1,224,7168]{2,1,0:T(8,128)(2,1)}, bf16[1,224,7168]{2,1,0:T(8,128)(2,1)}, bf16[512,256]{1,0:T(8...) custom-call(s32[8,128]{1,0:T(8,128)} %bitcast.6, s32[8,128]{1,0:T(8,128)} %bitcast.7, ...), custom_call_target="tpu_custom_call" | custom-call | tf_op jit(solution)/shard_map/routed_backward/pallas_call | solution.py:791
  175.5 8.9 %finish.1 = (bf16[128,7168]{1,0:T(8,128)(2,1)}, f32[8,128]{1,0:T(8,128)}, bf16[1,224,7168]{2,1,0:T(8,128)(2,1)}, bf16[1,224,7168]{2,1,0:T(8,128)(2,1)}, bf16[1,224,7168]{2,1,0:T(8,128)(2,1)}) custom-call(bf16[512,256]{1,0:T(8,128)(2,1)} %get-tuple-element.16.placet_hbm, f32[8,128]{1,0:T(8,128)} %get-tuple-element.17.gg_in, bf16[7,256,256]{2,1,0:T(8,128)(2,1)} %bitcast.5, ...), custom_call_target="tpu_custom_call" | custom-call | tf_op jit(solution)/shard_map/finish/pallas_call | solution.py:863

commit v5 on v4

--- a/solution.py
+++ b/solution.py
@@ -15,7 +15,8 @@
 CHUNKS = 2 * STAGES
 UNITS = 2 * CHUNKS
 GATHER_LAG = (2, 4, 6)
-REDUCE_LAG = (4, 8, 12)
+RING = 14
+REDUCE_LAG = (4, 8, 11)
 GRADS_LAG = 4
 PAD = 256
 MESH = pl.DeviceIdType.MESH
@@ -268,11 +269,11 @@
 
     def ag_copy(u, s, piece, to_n):
         ref = xbuf.at[u, piece]
-        return remote(ref, ref, ag_s.at[u // 7], ag_r.at[u, s], w, to_n)
+        return remote(ref, ref, ag_s.at[u // 7], ag_r.at[u % RING, s], w, to_n)
 
     def ag_half(u, s, piece, lower, to_n):
         ref = xbuf.at[u, piece, pl.ds(0 if lower else 32, 32)]
-        return remote(ref, ref, ag_s.at[u // 7], ag_r.at[u, s], w, to_n)
+        return remote(ref, ref, ag_s.at[u // 7], ag_r.at[u % RING, s], w, to_n)
 
     part = functools.partial
 
@@ -368,12 +369,12 @@
         def _():
             @pl.when(gather_is_b(u1))
             def _():
-                landed(xbuf.at[u1, pl.ds(0, 2)], ag_r.at[u1, 0])
+                landed(xbuf.at[u1, pl.ds(0, 2)], ag_r.at[u1 % RING, 0])
                 start_all(sends_b(u1)[1])
 
             @pl.when(jnp.logical_not(gather_is_b(u1)))
             def _():
-                landed(xbuf.at[u1, 0], ag_r.at[u1, 0])
+                landed(xbuf.at[u1, 0], ag_r.at[u1 % RING, 0])
                 start_all(sends_a(u1)[1])
 
         u2 = t - lag2
@@ -382,12 +383,12 @@
         def _():
             @pl.when(gather_is_b(u2))
             def _():
-                landed(xbuf.at[u2, 0], ag_r.at[u2, 1])
+                landed(xbuf.at[u2, 0], ag_r.at[u2 % RING, 1])
                 start_all(sends_b(u2)[2])
 
             @pl.when(jnp.logical_not(gather_is_b(u2)))
             def _():
-                landed(xbuf.at[u2, pl.ds(0, 4)], ag_r.at[u2, 1])
+                landed(xbuf.at[u2, pl.ds(0, 4)], ag_r.at[u2 % RING, 1])
                 start_all(sends_a(u2)[2])
 
         u3 = t - lag3
@@ -396,11 +397,11 @@
         def _():
             @pl.when(gather_is_b(u3))
             def _():
-                landed(xbuf.at[u3, pl.ds(0, 4)], ag_r.at[u3, 2])
+                landed(xbuf.at[u3, pl.ds(0, 4)], ag_r.at[u3 % RING, 2])
 
             @pl.when(jnp.logical_not(gather_is_b(u3)))
             def _():
-                landed(xbuf.at[u3, pl.ds(0, 2)], ag_r.at[u3, 2])
+                landed(xbuf.at[u3, pl.ds(0, 2)], ag_r.at[u3 % RING, 2])
 
             chunk = (u3 // 4) * 2 + u3 % 2
             is_cot = (u3 // 2) % 2 == 1
@@ -837,7 +838,7 @@
             dma((4,)),
             dma((4,)),
             dma((4,)),
-            dma((UNITS, 3)),
+            dma((RING, 3)),
             dma((2,)),
             dma((CHUNKS, 3)),
             dma((STAGES,)),

time: 185 us -> 189 us (1.022)
  Pallas kernels: 184 us -> 189 us
    pallas_call x1, Pallas kernels: 175 us -> 180 us  [per_device(): pl.pallas_call(kernel, out_shape=(sds(w_gate.shape, BF16), sds(w_up.shape...]
where the time goes in v5:
time: 189 us
  Pallas kernels  189 us (100%)
    pallas_call x1, Pallas kernels, per_device(): pl.pallas_call(kernel, out_shape=(sds(w_gate.shape, BF16), sds(w_up.shape...  180 us
    pallas_call x1, Pallas kernels, per_device(): pl.pallas_call(finish, in_specs=[any_spec] * 6, out_specs=(any_spec,) * 5...  8.94 us

profile of v5, /device:TPU:1, one launch (start us, length us, event | category | flops | bytes accessed | tf_op | source)
XLA Modules:
  0.0 189.2 jit_solution(17844779381876031251)
XLA Ops:
  0.6 179.6 %routed_backward.1 = (bf16[1,224,7168]{2,1,0:T(8,128)(2,1)}, bf16[1,224,7168]{2,1,0:T(8,128)(2,1)}, bf16[1,224,7168]{2,1,0:T(8,128)(2,1)}, bf16[512,256]{1,0:T(8...) custom-call(s32[8,128]{1,0:T(8,128)} %bitcast.6, s32[8,128]{1,0:T(8,128)} %bitcast.7, ...), custom_call_target="tpu_custom_call" | custom-call | tf_op jit(solution)/shard_map/routed_backward/pallas_call | solution.py:792
  180.3 8.9 %finish.1 = (bf16[128,7168]{1,0:T(8,128)(2,1)}, f32[8,128]{1,0:T(8,128)}, bf16[1,224,7168]{2,1,0:T(8,128)(2,1)}, bf16[1,224,7168]{2,1,0:T(8,128)(2,1)}, bf16[1,224,7168]{2,1,0:T(8,128)(2,1)}) custom-call(bf16[512,256]{1,0:T(8,128)(2,1)} %get-tuple-element.16.placet_hbm, f32[8,128]{1,0:T(8,128)} %get-tuple-element.17.gg_in, bf16[7,256,256]{2,1,0:T(8,128)(2,1)} %bitcast.5, ...), custom_call_target="tpu_custom_call" | custom-call | tf_op jit(solution)/shard_map/finish/pallas_call | solution.py:864

commit v6 on v5

--- a/solution.py
+++ b/solution.py
@@ -16,7 +16,7 @@
 UNITS = 2 * CHUNKS
 GATHER_LAG = (2, 4, 6)
 RING = 14
-REDUCE_LAG = (4, 8, 11)
+REDUCE_LAG = (4, 8, 12)
 GRADS_LAG = 4
 PAD = 256
 MESH = pl.DeviceIdType.MESH

time: 189 us -> 184 us (0.974)
  Pallas kernels: 189 us -> 183 us
    pallas_call x1, Pallas kernels: 180 us -> 174 us  [per_device(): pl.pallas_call(kernel, out_shape=(sds(w_gate.shape, BF16), sds(w_up.shape...]
where the time goes in v6:
time: 184 us
  Pallas kernels  183 us (99%)
    pallas_call x1, Pallas kernels, per_device(): pl.pallas_call(kernel, out_shape=(sds(w_gate.shape, BF16), sds(w_up.shape...  174 us
    pallas_call x1, Pallas kernels, per_device(): pl.pallas_call(finish, in_specs=[any_spec] * 6, out_specs=(any_spec,) * 5...  8.93 us

profile of v6, /device:TPU:1, one launch (start us, length us, event | category | flops | bytes accessed | tf_op | source)
XLA Modules:
  0.0 184.1 jit_solution(5356285605687024128)
XLA Ops:
  0.6 174.5 %routed_backward.1 = (bf16[1,224,7168]{2,1,0:T(8,128)(2,1)}, bf16[1,224,7168]{2,1,0:T(8,128)(2,1)}, bf16[1,224,7168]{2,1,0:T(8,128)(2,1)}, bf16[512,256]{1,0:T(8...) custom-call(s32[8,128]{1,0:T(8,128)} %bitcast.6, s32[8,128]{1,0:T(8,128)} %bitcast.7, ...), custom_call_target="tpu_custom_call" | custom-call | tf_op jit(solution)/shard_map/routed_backward/pallas_call | solution.py:792
  175.1 8.9 %finish.1 = (bf16[128,7168]{1,0:T(8,128)(2,1)}, f32[8,128]{1,0:T(8,128)}, bf16[1,224,7168]{2,1,0:T(8,128)(2,1)}, bf16[1,224,7168]{2,1,0:T(8,128)(2,1)}, bf16[1,224,7168]{2,1,0:T(8,128)(2,1)}) custom-call(bf16[512,256]{1,0:T(8,128)(2,1)} %get-tuple-element.16.placet_hbm, f32[8,128]{1,0:T(8,128)} %get-tuple-element.17.gg_in, bf16[7,256,256]{2,1,0:T(8,128)(2,1)} %bitcast.5, ...), custom_call_target="tpu_custom_call" | custom-call | tf_op jit(solution)/shard_map/finish/pallas_call | solution.py:864
